TPU v7x, 512 devices: a whole 4x4x16 slice. The times are simulated.
512 devices in a mesh: gx: 8 (over z_hi, x), gy: 16 (over z_lo, core), gz: 4 (over y).
Axes of the slice: x: 4, y: 4, z: 16 (z_hi: 2, z_lo: 8; z = z_hi * 8 + z_lo), core: 2. Of those that a mesh axis runs over, the one named last changes fastest.
Arguments:
- right_side: float32 [192, 384, 512], P('gx', 'gy', 'gz'), may hold values from -6 to 6
- reaction: float32 [192, 384, 512], P('gx', 'gy', 'gz'), may hold values from 0.05 to 2
- basis_x: float32 [40, 40], replicated, may hold values from -1 to 1
- basis_y: float32 [40, 40], replicated, may hold values from -1 to 1
- basis_z: float32 [144, 144], replicated, may hold values from -0.5 to 0.5
- eigen_x: float32 [40], replicated, may hold values from 0.5 to 6
- eigen_y: float32 [40], replicated, may hold values from 0.5 to 6
- eigen_z: float32 [144], replicated, may hold values from 0.5 to 6
Outputs:
- solution: float32 [192, 384, 512], P('gx', 'gy', 'gz')
All inputs are finite; a program needn't handle non-finite values.
Results may differ from a plain program's by a relative error of at most 0.0003.
Values sent between devices are 32-bit elements; how exact they have to be, the bound alone decides.
A program may use at most 64 MiB of HBM per device.

v0:
```python
import jax
import jax.numpy as jnp
from jax import lax
from jax.sharding import PartitionSpec as P

OV = 8


def padded_2(x, sides, width):
    for axis, dim in sides:
        peers, length = (lax.axis_size(axis), x.shape[dim])
        up = [(i, (i + 1) % peers) for i in range(peers - 1)]
        down = [(j, i) for i, j in up]
        last = lax.slice_in_dim(x, length - width, length, axis=dim)
        leading = lax.slice_in_dim(x, 0, width, axis=dim)
        before = lax.ppermute(last, axis, up)
        after = lax.ppermute(leading, axis, down)
        x = jnp.concatenate([before, x, after], axis=dim)
    return x


def stencil(padded, coefficient):
    center = padded[1:-1, 1:-1, 1:-1]
    sizes = center.shape
    total = coefficient * center
    weights = {1: 0.5, 2: 0.125, 3: 0.0625}
    for offset_x in (-1, 0, 1):
        for offset_y in (-1, 0, 1):
            for offset_z in (-1, 0, 1):
                count = abs(offset_x) + abs(offset_y) + abs(offset_z)
                if count == 0:
                    continue
                neighbour = padded[
                    1 + offset_x : 1 + offset_x + sizes[0],
                    1 + offset_y : 1 + offset_y + sizes[1],
                    1 + offset_z : 1 + offset_z + sizes[2],
                ]
                total = total + weights[count] * (center - neighbour)
    return total


def local_solve(block, basis_x, basis_y, basis_z, eigen_x, eigen_y, eigen_z):
    highest = lax.Precision.HIGHEST
    modes = jnp.einsum("ap,abc->pbc", basis_x, block, precision=highest)
    modes = jnp.einsum("bq,pbc->pqc", basis_y, modes, precision=highest)
    modes = jnp.einsum("cs,pqc->pqs", basis_z, modes, precision=highest)
    modes = modes / (eigen_x[:, None, None] + eigen_y[None, :, None] + eigen_z[None, None, :])
    back = jnp.einsum("ap,pqs->aqs", basis_x, modes, precision=highest)
    back = jnp.einsum("bq,aqs->abs", basis_y, back, precision=highest)
    back = jnp.einsum("cs,abs->abc", basis_z, back, precision=highest)
    return back


def settle(received, owned_count, dim):
    inner = lax.slice_in_dim(received, 2 * OV, 2 * OV + owned_count, axis=dim)
    lower = lax.slice_in_dim(received, 0, OV, axis=dim)
    upper = lax.slice_in_dim(received, received.shape[dim] - OV, received.shape[dim], axis=dim)
    low_pad = [(0, 0)] * 3
    low_pad[dim] = (0, owned_count - OV)
    high_pad = [(0, 0)] * 3
    high_pad[dim] = (owned_count - OV, 0)
    return inner + jnp.pad(lower, low_pad) + jnp.pad(upper, high_pad)


def fold_back(extended, owned_shape):
    received = padded_2(extended, (("gx", 0),), OV)
    folded = settle(received, owned_shape[0], 0)
    received = padded_2(folded, (("gy", 1),), OV)
    folded = settle(received, owned_shape[1], 1)
    received = padded_2(folded, (("gz", 2),), OV)
    return settle(received, owned_shape[2], 2)


def local(right_side, reaction, basis_x, basis_y, basis_z, eigen_x, eigen_y, eigen_z):
    owned_shape = right_side.shape
    tables = (basis_x, basis_y, basis_z, eigen_x, eigen_y, eigen_z)
    outer_rhs = padded_2(right_side, (("gx", 0), ("gy", 1), ("gz", 2)), OV)
    first = fold_back(local_solve(outer_rhs, *tables), owned_shape)
    layered = padded_2(first, (("gx", 0), ("gy", 1), ("gz", 2)), 1)
    residual = right_side - stencil(layered, reaction)
    outer_resid = padded_2(residual, (("gx", 0), ("gy", 1), ("gz", 2)), OV)
    solution = first + fold_back(local_solve(outer_resid, *tables), owned_shape)
    return solution


def solution(mesh):
    return jax.shard_map(
        local,
        mesh=mesh,
        in_specs=(P("gx", "gy", "gz"), P("gx", "gy", "gz"), P(), P(), P(), P(), P(), P()),
        out_specs=P("gx", "gy", "gz"),
        check_vma=False,
    )
```

profile of v0, /device:TPU:7, one launch (start us, length us, event | category | flops | bytes accessed | tf_op | source)
XLA Modules:
  0.0 291.7 jit_solution(13287309118813112)
XLA Ops:
  1.0 15.4 %collective-permute-start = (f32[8,24,128]{2,1,0:T(8,128)S(1)}, f32[8,24,128]{2,1,0:T(8,128)S(1)}, u32[]{:S(2)}, u32[]{:S(2)}) collective-permute-start(f32[8,24,128]{2,1,0:T(8,128)S(1)} %get-tuple-element.38), channel_id=1, source_target_pairs={{0,64},{64,128},{128,192},{192,256},{256,320},{320,384},{384,448},... | collective-permute-start | bytes 294920 | tf_op jit(solution)/shard_map/ppermute | solution.py:16
  16.4 1.9 collective-permute-start.1
  19.3 13.4 %collective-permute-done.1 = f32[8,24,128]{2,1,0:T(8,128)S(1)} collective-permute-done((f32[8,24,128]{2,1,0:T(8,128)S(1)}, f32[8,24,128]{2,1,0:T(8,128)S(1)}, u32[]{:S(2)}, u32[]{:S(2)}) %collective-permute-start.1) | collective-permute-done | bytes 98336 | tf_op jit(solution)/shard_map/ppermute | solution.py:17
  32.8 10.4 %collective-permute-start.2 = (f32[40,8,128]{2,1,0:T(8,128)S(1)}, f32[40,8,128]{2,1,0:T(8,128)S(1)}, u32[]{:S(2)}, u32[]{:S(2)}) collective-permute-start(f32[40,8,128]{2,1,0:T(8,128)S(1)} %get-tuple-element.23), channel_id=1, source_target_pairs={{0,4},{4,8},{8,12},{12,16},{16,20},{20,24},{24,28},{28,32},{32,36}... | collective-permute-start | bytes 491528 | tf_op jit(solution)/shard_map/ppermute | solution.py:16
  43.2 1.9 collective-permute-start.3
  45.4 4.4 %collective-permute-done.3 = f32[40,8,128]{2,1,0:T(8,128)S(1)} collective-permute-done((f32[40,8,128]{2,1,0:T(8,128)S(1)}, f32[40,8,128]{2,1,0:T(8,128)S(1)}, u32[]{:S(2)}, u32[]{:S(2)}) %collective-permute-start.3) | collective-permute-done | bytes 163872 | tf_op jit(solution)/shard_map/ppermute | solution.py:17
  52.0 4.0 %collective-permute-start.4 = (f32[40,40,8]{1,2,0:T(8,128)S(1)}, f32[40,40,8]{1,2,0:T(8,128)S(1)}, u32[]{:S(2)}, u32[]{:S(2)}) collective-permute-start(f32[40,40,8]{1,2,0:T(8,128)S(1)} %copy.44), channel_id=1, source_target_pairs={{0,1},{1,2},{2,3},{4,5},{5,6},{6,7},{8,9},{9,10},{10,11},{12,13},{... | collective-permute-start | bytes 153608 | tf_op jit(solution)/shard_map/ppermute | solution.py:16
  56.3 2.0 collective-permute-done.4
  59.0 2.1 fusion.37
  61.0 2.1 fusion.26
  64.6 2.1 fusion.28
  66.7 2.1 fusion.22
  72.3 3.4 %collective-permute-start.7 = (f32[8,40,144]{2,1,0:T(8,128)S(1)}, f32[8,40,144]{2,1,0:T(8,128)S(1)}, u32[]{:S(2)}, u32[]{:S(2)}) collective-permute-start(f32[8,40,144]{2,1,0:T(8,128)S(1)} %get-tuple-element.8), channel_id=1, source_target_pairs={{64,0},{128,64},{192,128},{256,192},{320,256},{384,320},{448,384},... | collective-permute-start | bytes 552968 | tf_op jit(solution)/shard_map/ppermute | solution.py:17
  75.7 4.3 %collective-permute-done.6 = f32[8,40,144]{2,1,0:T(8,128)S(1)} collective-permute-done((f32[8,40,144]{2,1,0:T(8,128)S(1)}, f32[8,40,144]{2,1,0:T(8,128)S(1)}, u32[]{:S(2)}, u32[]{:S(2)}) %collective-permute-start.6) | collective-permute-done | bytes 184352 | tf_op jit(solution)/shard_map/ppermute | solution.py:16
  80.0 13.0 %collective-permute-done.7 = f32[8,40,144]{2,1,0:T(8,128)S(1)} collective-permute-done((f32[8,40,144]{2,1,0:T(8,128)S(1)}, f32[8,40,144]{2,1,0:T(8,128)S(1)}, u32[]{:S(2)}, u32[]{:S(2)}) %collective-permute-start.7) | collective-permute-done | bytes 184352 | tf_op jit(solution)/shard_map/ppermute | solution.py:17
  93.1 19.9 %collective-permute-start.8 = (f32[24,8,144]{2,1,0:T(8,128)S(1)}, f32[24,8,144]{2,1,0:T(8,128)S(1)}, u32[]{:S(2)}, u32[]{:S(2)}) collective-permute-start(f32[24,8,144]{2,1,0:T(8,128)S(1)} %get-tuple-element.11), channel_id=1, source_target_pairs={{0,4},{4,8},{8,12},{12,16},{16,20},{20,24},{24,28},{28,32},{32,36}... | collective-permute-start | bytes 331784 | tf_op jit(solution)/shard_map/ppermute | solution.py:16
  113.0 2.1 collective-permute-start.9
  115.6 4.4 %collective-permute-done.9 = f32[24,8,144]{2,1,0:T(8,128)S(1)} collective-permute-done((f32[24,8,144]{2,1,0:T(8,128)S(1)}, f32[24,8,144]{2,1,0:T(8,128)S(1)}, u32[]{:S(2)}, u32[]{:S(2)}) %collective-permute-start.9) | collective-permute-done | bytes 110624 | tf_op jit(solution)/shard_map/ppermute | solution.py:17
  120.2 4.1 %collective-permute-start.10 = (f32[24,24,8]{2,1,0:T(8,128)S(1)}, f32[24,24,8]{2,1,0:T(8,128)S(1)}, u32[]{:S(2)}, u32[]{:S(2)}) collective-permute-start(f32[24,24,8]{2,1,0:T(8,128)S(1)} %get-tuple-element.19), channel_id=1, source_target_pairs={{0,1},{1,2},{2,3},{4,5},{5,6},{6,7},{8,9},{9,10},{10,11},{12,13},{... | collective-permute-start | bytes 55304 | tf_op jit(solution)/shard_map/ppermute | solution.py:16
  125.6 2.5 collective-permute-done.10
  128.1 4.1 %collective-permute-done.11 = f32[24,24,8]{2,1,0:T(8,128)S(1)} collective-permute-done((f32[24,24,8]{2,1,0:T(8,128)S(1)}, f32[24,24,8]{2,1,0:T(8,128)S(1)}, u32[]{:S(2)}, u32[]{:S(2)}) %collective-permute-start.11) | collective-permute-done | bytes 18464 | tf_op jit(solution)/shard_map/ppermute | solution.py:17
  134.4 3.4 %collective-permute-start.13 = (f32[1,24,128]{2,1,0:T(8,128)S(1)}, f32[1,24,128]{2,1,0:T(8,128)S(1)}, u32[]{:S(2)}, u32[]{:S(2)}) collective-permute-start(f32[1,24,128]{2,1,0:T(8,128)S(1)} %get-tuple-element.36), channel_id=1, source_target_pairs={{64,0},{128,64},{192,128},{256,192},{320,256},{384,320},{448,384},... | collective-permute-start | bytes 36872 | tf_op jit(solution)/shard_map/ppermute | solution.py:17
  137.8 11.9 %collective-permute-done.13 = f32[1,24,128]{2,1,0:T(8,128)S(1)} collective-permute-done((f32[1,24,128]{2,1,0:T(8,128)S(1)}, f32[1,24,128]{2,1,0:T(8,128)S(1)}, u32[]{:S(2)}, u32[]{:S(2)}) %collective-permute-start.13) | collective-permute-done | bytes 12320 | tf_op jit(solution)/shard_map/ppermute | solution.py:17
  149.7 3.9 %collective-permute-start.14 = (f32[26,1,128]{2,1,0:T(1,128)S(1)}, f32[26,1,128]{2,1,0:T(1,128)S(1)}, u32[]{:S(2)}, u32[]{:S(2)}) collective-permute-start(f32[26,1,128]{2,1,0:T(1,128)S(1)} %get-tuple-element.31), channel_id=1, source_target_pairs={{0,4},{4,8},{8,12},{12,16},{16,20},{20,24},{24,28},{28,32},{32,36}... | collective-permute-start | bytes 39944 | tf_op jit(solution)/shard_map/ppermute | solution.py:16
  155.5 3.1 %collective-permute-done.15 = f32[26,1,128]{2,1,0:T(1,128)S(1)} collective-permute-done((f32[26,1,128]{2,1,0:T(1,128)S(1)}, f32[26,1,128]{2,1,0:T(1,128)S(1)}, u32[]{:S(2)}, u32[]{:S(2)}) %collective-permute-start.15) | collective-permute-done | bytes 13344 | tf_op jit(solution)/shard_map/ppermute | solution.py:17
  158.9 3.2 %collective-permute-start.16 = (f32[26,26,1]{2,1,0:T(8,128)S(1)}, f32[26,26,1]{2,1,0:T(8,128)S(1)}, u32[]{:S(2)}, u32[]{:S(2)}) collective-permute-start(f32[26,26,1]{2,1,0:T(8,128)S(1)} %get-tuple-element.25), channel_id=1, source_target_pairs={{0,1},{1,2},{2,3},{4,5},{5,6},{6,7},{8,9},{9,10},{10,11},{12,13},{... | collective-permute-start | bytes 8120 | tf_op jit(solution)/shard_map/ppermute | solution.py:16
  163.5 6.7 %collective-permute-done.16 = f32[26,26,1]{2,1,0:T(8,128)S(1)} collective-permute-done((f32[26,26,1]{2,1,0:T(8,128)S(1)}, f32[26,26,1]{2,1,0:T(8,128)S(1)}, u32[]{:S(2)}, u32[]{:S(2)}) %collective-permute-start.16) | collective-permute-done | bytes 2736 | tf_op jit(solution)/shard_map/ppermute | solution.py:16
  170.2 4.1 %collective-permute-done.17 = f32[26,26,1]{2,1,0:T(8,128)S(1)} collective-permute-done((f32[26,26,1]{2,1,0:T(8,128)S(1)}, f32[26,26,1]{2,1,0:T(8,128)S(1)}, u32[]{:S(2)}, u32[]{:S(2)}) %collective-permute-start.17) | collective-permute-done | bytes 2736 | tf_op jit(solution)/shard_map/ppermute | solution.py:17
  177.8 3.4 %collective-permute-start.19 = (f32[8,24,128]{2,1,0:T(8,128)S(1)}, f32[8,24,128]{2,1,0:T(8,128)S(1)}, u32[]{:S(2)}, u32[]{:S(2)}) collective-permute-start(f32[8,24,128]{2,1,0:T(8,128)S(1)} %get-tuple-element.34), channel_id=1, source_target_pairs={{64,0},{128,64},{192,128},{256,192},{320,256},{384,320},{448,384},... | collective-permute-start | bytes 294920 | tf_op jit(solution)/shard_map/ppermute | solution.py:17
  182.4 12.8 %collective-permute-done.19 = f32[8,24,128]{2,1,0:T(8,128)S(1)} collective-permute-done((f32[8,24,128]{2,1,0:T(8,128)S(1)}, f32[8,24,128]{2,1,0:T(8,128)S(1)}, u32[]{:S(2)}, u32[]{:S(2)}) %collective-permute-start.19) | collective-permute-done | bytes 98336 | tf_op jit(solution)/shard_map/ppermute | solution.py:17
  195.2 3.7 %collective-permute-start.20 = (f32[40,8,128]{2,1,0:T(8,128)S(1)}, f32[40,8,128]{2,1,0:T(8,128)S(1)}, u32[]{:S(2)}, u32[]{:S(2)}) collective-permute-start(f32[40,8,128]{2,1,0:T(8,128)S(1)} %get-tuple-element.21), channel_id=1, source_target_pairs={{0,4},{4,8},{8,12},{12,16},{16,20},{20,24},{24,28},{28,32},{32,36}... | collective-permute-start | bytes 491528 | tf_op jit(solution)/shard_map/ppermute | solution.py:16
  201.1 4.4 %collective-permute-done.21 = f32[40,8,128]{2,1,0:T(8,128)S(1)} collective-permute-done((f32[40,8,128]{2,1,0:T(8,128)S(1)}, f32[40,8,128]{2,1,0:T(8,128)S(1)}, u32[]{:S(2)}, u32[]{:S(2)}) %collective-permute-start.21) | collective-permute-done | bytes 163872 | tf_op jit(solution)/shard_map/ppermute | solution.py:17
  206.1 3.2 %collective-permute-start.22 = (f32[40,40,8]{1,2,0:T(8,128)S(1)}, f32[40,40,8]{1,2,0:T(8,128)S(1)}, u32[]{:S(2)}, u32[]{:S(2)}) collective-permute-start(f32[40,40,8]{1,2,0:T(8,128)S(1)} %copy.26), channel_id=1, source_target_pairs={{0,1},{1,2},{2,3},{4,5},{5,6},{6,7},{8,9},{9,10},{10,11},{12,13},{... | collective-permute-start | bytes 153608 | tf_op jit(solution)/shard_map/ppermute | solution.py:16
  211.9 3.8 %collective-permute-done.23 = f32[40,40,8]{1,2,0:T(8,128)S(1)} collective-permute-done((f32[40,40,8]{1,2,0:T(8,128)S(1)}, f32[40,40,8]{1,2,0:T(8,128)S(1)}, u32[]{:S(2)}, u32[]{:S(2)}) %collective-permute-start.23) | collective-permute-done | bytes 51232 | tf_op jit(solution)/shard_map/ppermute | solution.py:17
  216.7 2.1 fusion.31
  218.8 2.1 fusion.18
  222.3 2.1 fusion.34
  224.4 2.1 fusion.14
  228.1 1.9 collective-permute-start.24
  230.0 3.4 %collective-permute-start.25 = (f32[8,40,144]{2,1,0:T(8,128)S(1)}, f32[8,40,144]{2,1,0:T(8,128)S(1)}, u32[]{:S(2)}, u32[]{:S(2)}) collective-permute-start(f32[8,40,144]{2,1,0:T(8,128)S(1)} %get-tuple-element.6), channel_id=1, source_target_pairs={{64,0},{128,64},{192,128},{256,192},{320,256},{384,320},{448,384},... | collective-permute-start | bytes 552968 | tf_op jit(solution)/shard_map/ppermute | solution.py:17
  233.4 4.6 %collective-permute-done.24 = f32[8,40,144]{2,1,0:T(8,128)S(1)} collective-permute-done((f32[8,40,144]{2,1,0:T(8,128)S(1)}, f32[8,40,144]{2,1,0:T(8,128)S(1)}, u32[]{:S(2)}, u32[]{:S(2)}) %collective-permute-start.24) | collective-permute-done | bytes 184352 | tf_op jit(solution)/shard_map/ppermute | solution.py:16
  237.9 13.1 %collective-permute-done.25 = f32[8,40,144]{2,1,0:T(8,128)S(1)} collective-permute-done((f32[8,40,144]{2,1,0:T(8,128)S(1)}, f32[8,40,144]{2,1,0:T(8,128)S(1)}, u32[]{:S(2)}, u32[]{:S(2)}) %collective-permute-start.25) | collective-permute-done | bytes 184352 | tf_op jit(solution)/shard_map/ppermute | solution.py:17
  251.2 22.7 %collective-permute-start.26 = (f32[24,8,144]{2,1,0:T(8,128)S(1)}, f32[24,8,144]{2,1,0:T(8,128)S(1)}, u32[]{:S(2)}, u32[]{:S(2)}) collective-permute-start(f32[24,8,144]{2,1,0:T(8,128)S(1)} %get-tuple-element.9), channel_id=1, source_target_pairs={{0,4},{4,8},{8,12},{12,16},{16,20},{20,24},{24,28},{28,32},{32,36}... | collective-permute-start | bytes 331784 | tf_op jit(solution)/shard_map/ppermute | solution.py:16
  273.8 1.9 collective-permute-start.27
  276.4 4.4 %collective-permute-done.27 = f32[24,8,144]{2,1,0:T(8,128)S(1)} collective-permute-done((f32[24,8,144]{2,1,0:T(8,128)S(1)}, f32[24,8,144]{2,1,0:T(8,128)S(1)}, u32[]{:S(2)}, u32[]{:S(2)}) %collective-permute-start.27) | collective-permute-done | bytes 110624 | tf_op jit(solution)/shard_map/ppermute | solution.py:17
  281.1 1.9 collective-permute-start.28
  284.3 2.3 collective-permute-done.28
  286.6 4.1 %collective-permute-done.29 = f32[24,24,8]{2,1,0:T(8,128)S(1)} collective-permute-done((f32[24,24,8]{2,1,0:T(8,128)S(1)}, f32[24,24,8]{2,1,0:T(8,128)S(1)}, u32[]{:S(2)}, u32[]{:S(2)}) %collective-permute-start.29) | collective-permute-done | bytes 18464 | tf_op jit(solution)/shard_map/ppermute | solution.py:17
  (81 shorter events, 35.3 us)
Async XLA Ops:
  0.0 63.1 %copy-start = (f32[144,144]{1,0:T(8,128)S(1)}, f32[144,144]{1,0:T(8,128)}, u32[]{:S(2)}) copy-start(f32[144,144]{1,0:T(8,128)} %param.12) | copy-start | bytes 248836
  1.0 17.3 %collective-permute-start = (f32[8,24,128]{2,1,0:T(8,128)S(1)}, f32[8,24,128]{2,1,0:T(8,128)S(1)}, u32[]{:S(2)}, u32[]{:S(2)}) collective-permute-start(f32[8,24,128]{2,1,0:T(8,128)S(1)} %get-tuple-element.38), channel_id=1, source_target_pairs={{0,64},{64,128},{128,192},{192,256},{256,320},{320,384},{384,448},... | collective-permute-start | bytes 294920 | tf_op jit(solution)/shard_map/ppermute | solution.py:16
  16.4 16.4 %collective-permute-start.1 = (f32[8,24,128]{2,1,0:T(8,128)S(1)}, f32[8,24,128]{2,1,0:T(8,128)S(1)}, u32[]{:S(2)}, u32[]{:S(2)}) collective-permute-start(f32[8,24,128]{2,1,0:T(8,128)S(1)} %get-tuple-element.37), channel_id=1, source_target_pairs={{64,0},{128,64},{192,128},{256,192},{320,256},{384,320},{448,384},... | collective-permute-start | bytes 294920 | tf_op jit(solution)/shard_map/ppermute | solution.py:17
  32.8 12.6 %collective-permute-start.2 = (f32[40,8,128]{2,1,0:T(8,128)S(1)}, f32[40,8,128]{2,1,0:T(8,128)S(1)}, u32[]{:S(2)}, u32[]{:S(2)}) collective-permute-start(f32[40,8,128]{2,1,0:T(8,128)S(1)} %get-tuple-element.23), channel_id=1, source_target_pairs={{0,4},{4,8},{8,12},{12,16},{16,20},{20,24},{24,28},{28,32},{32,36}... | collective-permute-start | bytes 491528 | tf_op jit(solution)/shard_map/ppermute | solution.py:16
  43.2 6.6 %collective-permute-start.3 = (f32[40,8,128]{2,1,0:T(8,128)S(1)}, f32[40,8,128]{2,1,0:T(8,128)S(1)}, u32[]{:S(2)}, u32[]{:S(2)}) collective-permute-start(f32[40,8,128]{2,1,0:T(8,128)S(1)} %get-tuple-element.24), channel_id=1, source_target_pairs={{4,0},{8,4},{12,8},{16,12},{20,16},{24,20},{28,24},{32,28},{36,32}... | collective-permute-start | bytes 491528 | tf_op jit(solution)/shard_map/ppermute | solution.py:17
  50.2 5.9 %copy-start.5 = (f32[40]{0:T(128)S(1)}, f32[40]{0:T(128)}, u32[]{:S(2)}) copy-start(f32[40]{0:T(128)} %param.14) | copy-start | bytes 484
  50.2 5.9 %copy-start.6 = (f32[40]{0:T(128)S(1)}, f32[40]{0:T(128)}, u32[]{:S(2)}) copy-start(f32[40]{0:T(128)} %param.13) | copy-start | bytes 484
  50.7 7.9 %collective-permute-start.5 = (f32[40,40,8]{1,2,0:T(8,128)S(1)}, f32[40,40,8]{1,2,0:T(8,128)S(1)}, u32[]{:S(2)}, u32[]{:S(2)}) collective-permute-start(f32[40,40,8]{1,2,0:T(8,128)S(1)} %copy.45), channel_id=1, source_target_pairs={{1,0},{2,1},{3,2},{5,4},{6,5},{7,6},{9,8},{10,9},{11,10},{13,12},{... | collective-permute-start | bytes 153608 | tf_op jit(solution)/shard_map/ppermute | solution.py:17
  52.0 6.2 %collective-permute-start.4 = (f32[40,40,8]{1,2,0:T(8,128)S(1)}, f32[40,40,8]{1,2,0:T(8,128)S(1)}, u32[]{:S(2)}, u32[]{:S(2)}) collective-permute-start(f32[40,40,8]{1,2,0:T(8,128)S(1)} %copy.44), channel_id=1, source_target_pairs={{0,1},{1,2},{2,3},{4,5},{5,6},{6,7},{8,9},{9,10},{10,11},{12,13},{... | collective-permute-start | bytes 153608 | tf_op jit(solution)/shard_map/ppermute | solution.py:16
  56.1 2.8 copy-start.2
  58.9 2.1 copy-start.3
  61.0 2.1 copy-start.7
  70.4 9.6 %collective-permute-start.6 = (f32[8,40,144]{2,1,0:T(8,128)S(1)}, f32[8,40,144]{2,1,0:T(8,128)S(1)}, u32[]{:S(2)}, u32[]{:S(2)}) collective-permute-start(f32[8,40,144]{2,1,0:T(8,128)S(1)} %get-tuple-element.7), channel_id=1, source_target_pairs={{0,64},{64,128},{128,192},{192,256},{256,320},{320,384},{384,448},... | collective-permute-start | bytes 552968 | tf_op jit(solution)/shard_map/ppermute | solution.py:16
  72.3 20.6 %collective-permute-start.7 = (f32[8,40,144]{2,1,0:T(8,128)S(1)}, f32[8,40,144]{2,1,0:T(8,128)S(1)}, u32[]{:S(2)}, u32[]{:S(2)}) collective-permute-start(f32[8,40,144]{2,1,0:T(8,128)S(1)} %get-tuple-element.8), channel_id=1, source_target_pairs={{64,0},{128,64},{192,128},{256,192},{320,256},{384,320},{448,384},... | collective-permute-start | bytes 552968 | tf_op jit(solution)/shard_map/ppermute | solution.py:17
  93.1 22.5 %collective-permute-start.8 = (f32[24,8,144]{2,1,0:T(8,128)S(1)}, f32[24,8,144]{2,1,0:T(8,128)S(1)}, u32[]{:S(2)}, u32[]{:S(2)}) collective-permute-start(f32[24,8,144]{2,1,0:T(8,128)S(1)} %get-tuple-element.11), channel_id=1, source_target_pairs={{0,4},{4,8},{8,12},{12,16},{16,20},{20,24},{24,28},{28,32},{32,36}... | collective-permute-start | bytes 331784 | tf_op jit(solution)/shard_map/ppermute | solution.py:16
  113.0 7.0 %collective-permute-start.9 = (f32[24,8,144]{2,1,0:T(8,128)S(1)}, f32[24,8,144]{2,1,0:T(8,128)S(1)}, u32[]{:S(2)}, u32[]{:S(2)}) collective-permute-start(f32[24,8,144]{2,1,0:T(8,128)S(1)} %get-tuple-element.12), channel_id=1, source_target_pairs={{4,0},{8,4},{12,8},{16,12},{20,16},{24,20},{28,24},{32,28},{36,32}... | collective-permute-start | bytes 331784 | tf_op jit(solution)/shard_map/ppermute | solution.py:17
  120.2 7.9 %collective-permute-start.10 = (f32[24,24,8]{2,1,0:T(8,128)S(1)}, f32[24,24,8]{2,1,0:T(8,128)S(1)}, u32[]{:S(2)}, u32[]{:S(2)}) collective-permute-start(f32[24,24,8]{2,1,0:T(8,128)S(1)} %get-tuple-element.19), channel_id=1, source_target_pairs={{0,1},{1,2},{2,3},{4,5},{5,6},{6,7},{8,9},{9,10},{10,11},{12,13},{... | collective-permute-start | bytes 55304 | tf_op jit(solution)/shard_map/ppermute | solution.py:16
  124.3 7.9 %collective-permute-start.11 = (f32[24,24,8]{2,1,0:T(8,128)S(1)}, f32[24,24,8]{2,1,0:T(8,128)S(1)}, u32[]{:S(2)}, u32[]{:S(2)}) collective-permute-start(f32[24,24,8]{2,1,0:T(8,128)S(1)} %get-tuple-element.20), channel_id=1, source_target_pairs={{1,0},{2,1},{3,2},{5,4},{6,5},{7,6},{9,8},{10,9},{11,10},{13,12},{... | collective-permute-start | bytes 55304 | tf_op jit(solution)/shard_map/ppermute | solution.py:17
  132.5 5.3 %collective-permute-start.12 = (f32[1,24,128]{2,1,0:T(8,128)S(1)}, f32[1,24,128]{2,1,0:T(8,128)S(1)}, u32[]{:S(2)}, u32[]{:S(2)}) collective-permute-start(f32[1,24,128]{2,1,0:T(8,128)S(1)} %get-tuple-element.35), channel_id=1, source_target_pairs={{0,64},{64,128},{128,192},{192,256},{256,320},{320,384},{384,448},... | collective-permute-start | bytes 36872 | tf_op jit(solution)/shard_map/ppermute | solution.py:16
  134.4 15.3 %collective-permute-start.13 = (f32[1,24,128]{2,1,0:T(8,128)S(1)}, f32[1,24,128]{2,1,0:T(8,128)S(1)}, u32[]{:S(2)}, u32[]{:S(2)}) collective-permute-start(f32[1,24,128]{2,1,0:T(8,128)S(1)} %get-tuple-element.36), channel_id=1, source_target_pairs={{64,0},{128,64},{192,128},{256,192},{320,256},{384,320},{448,384},... | collective-permute-start | bytes 36872 | tf_op jit(solution)/shard_map/ppermute | solution.py:17
  149.7 5.9 %collective-permute-start.14 = (f32[26,1,128]{2,1,0:T(1,128)S(1)}, f32[26,1,128]{2,1,0:T(1,128)S(1)}, u32[]{:S(2)}, u32[]{:S(2)}) collective-permute-start(f32[26,1,128]{2,1,0:T(1,128)S(1)} %get-tuple-element.31), channel_id=1, source_target_pairs={{0,4},{4,8},{8,12},{12,16},{16,20},{20,24},{24,28},{28,32},{32,36}... | collective-permute-start | bytes 39944 | tf_op jit(solution)/shard_map/ppermute | solution.py:16
  153.6 5.0 %collective-permute-start.15 = (f32[26,1,128]{2,1,0:T(1,128)S(1)}, f32[26,1,128]{2,1,0:T(1,128)S(1)}, u32[]{:S(2)}, u32[]{:S(2)}) collective-permute-start(f32[26,1,128]{2,1,0:T(1,128)S(1)} %get-tuple-element.32), channel_id=1, source_target_pairs={{4,0},{8,4},{12,8},{16,12},{20,16},{24,20},{28,24},{32,28},{36,32}... | collective-permute-start | bytes 39944 | tf_op jit(solution)/shard_map/ppermute | solution.py:17
  158.9 11.3 %collective-permute-start.16 = (f32[26,26,1]{2,1,0:T(8,128)S(1)}, f32[26,26,1]{2,1,0:T(8,128)S(1)}, u32[]{:S(2)}, u32[]{:S(2)}) collective-permute-start(f32[26,26,1]{2,1,0:T(8,128)S(1)} %get-tuple-element.25), channel_id=1, source_target_pairs={{0,1},{1,2},{2,3},{4,5},{5,6},{6,7},{8,9},{9,10},{10,11},{12,13},{... | collective-permute-start | bytes 8120 | tf_op jit(solution)/shard_map/ppermute | solution.py:16
  162.1 12.2 %collective-permute-start.17 = (f32[26,26,1]{2,1,0:T(8,128)S(1)}, f32[26,26,1]{2,1,0:T(8,128)S(1)}, u32[]{:S(2)}, u32[]{:S(2)}) collective-permute-start(f32[26,26,1]{2,1,0:T(8,128)S(1)} %get-tuple-element.26), channel_id=1, source_target_pairs={{1,0},{2,1},{3,2},{5,4},{6,5},{7,6},{9,8},{10,9},{11,10},{13,12},{... | collective-permute-start | bytes 8120 | tf_op jit(solution)/shard_map/ppermute | solution.py:17
  163.5 11.3 %copy-start.1 = (f32[24,24,128]{2,1,0:T(8,128)S(1)}, f32[24,24,128]{2,1,0:T(8,128)}, u32[]{:S(2)}) copy-start(f32[24,24,128]{2,1,0:T(8,128)} %param.8) | copy-start | bytes 884740
  163.5 11.3 %copy-start.4 = (f32[24,24,128]{2,1,0:T(8,128)S(1)}, f32[24,24,128]{2,1,0:T(8,128)}, u32[]{:S(2)}) copy-start(f32[24,24,128]{2,1,0:T(8,128)} %param.9) | copy-start | bytes 884740
  175.8 6.5 %collective-permute-start.18 = (f32[8,24,128]{2,1,0:T(8,128)S(1)}, f32[8,24,128]{2,1,0:T(8,128)S(1)}, u32[]{:S(2)}, u32[]{:S(2)}) collective-permute-start(f32[8,24,128]{2,1,0:T(8,128)S(1)} %get-tuple-element.33), channel_id=1, source_target_pairs={{0,64},{64,128},{128,192},{192,256},{256,320},{320,384},{384,448},... | collective-permute-start | bytes 294920 | tf_op jit(solution)/shard_map/ppermute | solution.py:16
  177.8 17.4 %collective-permute-start.19 = (f32[8,24,128]{2,1,0:T(8,128)S(1)}, f32[8,24,128]{2,1,0:T(8,128)S(1)}, u32[]{:S(2)}, u32[]{:S(2)}) collective-permute-start(f32[8,24,128]{2,1,0:T(8,128)S(1)} %get-tuple-element.34), channel_id=1, source_target_pairs={{64,0},{128,64},{192,128},{256,192},{320,256},{384,320},{448,384},... | collective-permute-start | bytes 294920 | tf_op jit(solution)/shard_map/ppermute | solution.py:17
  195.2 6.0 %collective-permute-start.20 = (f32[40,8,128]{2,1,0:T(8,128)S(1)}, f32[40,8,128]{2,1,0:T(8,128)S(1)}, u32[]{:S(2)}, u32[]{:S(2)}) collective-permute-start(f32[40,8,128]{2,1,0:T(8,128)S(1)} %get-tuple-element.21), channel_id=1, source_target_pairs={{0,4},{4,8},{8,12},{12,16},{16,20},{20,24},{24,28},{28,32},{32,36}... | collective-permute-start | bytes 491528 | tf_op jit(solution)/shard_map/ppermute | solution.py:16
  198.9 6.6 %collective-permute-start.21 = (f32[40,8,128]{2,1,0:T(8,128)S(1)}, f32[40,8,128]{2,1,0:T(8,128)S(1)}, u32[]{:S(2)}, u32[]{:S(2)}) collective-permute-start(f32[40,8,128]{2,1,0:T(8,128)S(1)} %get-tuple-element.22), channel_id=1, source_target_pairs={{4,0},{8,4},{12,8},{16,12},{20,16},{24,20},{28,24},{32,28},{36,32}... | collective-permute-start | bytes 491528 | tf_op jit(solution)/shard_map/ppermute | solution.py:17
  206.1 5.5 %collective-permute-start.22 = (f32[40,40,8]{1,2,0:T(8,128)S(1)}, f32[40,40,8]{1,2,0:T(8,128)S(1)}, u32[]{:S(2)}, u32[]{:S(2)}) collective-permute-start(f32[40,40,8]{1,2,0:T(8,128)S(1)} %copy.26), channel_id=1, source_target_pairs={{0,1},{1,2},{2,3},{4,5},{5,6},{6,7},{8,9},{9,10},{10,11},{12,13},{... | collective-permute-start | bytes 153608 | tf_op jit(solution)/shard_map/ppermute | solution.py:16
  209.6 6.1 %collective-permute-start.23 = (f32[40,40,8]{1,2,0:T(8,128)S(1)}, f32[40,40,8]{1,2,0:T(8,128)S(1)}, u32[]{:S(2)}, u32[]{:S(2)}) collective-permute-start(f32[40,40,8]{1,2,0:T(8,128)S(1)} %copy.27), channel_id=1, source_target_pairs={{1,0},{2,1},{3,2},{5,4},{6,5},{7,6},{9,8},{10,9},{11,10},{13,12},{... | collective-permute-start | bytes 153608 | tf_op jit(solution)/shard_map/ppermute | solution.py:17
  228.1 9.9 %collective-permute-start.24 = (f32[8,40,144]{2,1,0:T(8,128)S(1)}, f32[8,40,144]{2,1,0:T(8,128)S(1)}, u32[]{:S(2)}, u32[]{:S(2)}) collective-permute-start(f32[8,40,144]{2,1,0:T(8,128)S(1)} %get-tuple-element.5), channel_id=1, source_target_pairs={{0,64},{64,128},{128,192},{192,256},{256,320},{320,384},{384,448},... | collective-permute-start | bytes 552968 | tf_op jit(solution)/shard_map/ppermute | solution.py:16
  230.0 21.0 %collective-permute-start.25 = (f32[8,40,144]{2,1,0:T(8,128)S(1)}, f32[8,40,144]{2,1,0:T(8,128)S(1)}, u32[]{:S(2)}, u32[]{:S(2)}) collective-permute-start(f32[8,40,144]{2,1,0:T(8,128)S(1)} %get-tuple-element.6), channel_id=1, source_target_pairs={{64,0},{128,64},{192,128},{256,192},{320,256},{384,320},{448,384},... | collective-permute-start | bytes 552968 | tf_op jit(solution)/shard_map/ppermute | solution.py:17
  251.2 25.3 %collective-permute-start.26 = (f32[24,8,144]{2,1,0:T(8,128)S(1)}, f32[24,8,144]{2,1,0:T(8,128)S(1)}, u32[]{:S(2)}, u32[]{:S(2)}) collective-permute-start(f32[24,8,144]{2,1,0:T(8,128)S(1)} %get-tuple-element.9), channel_id=1, source_target_pairs={{0,4},{4,8},{8,12},{12,16},{16,20},{20,24},{24,28},{28,32},{32,36}... | collective-permute-start | bytes 331784 | tf_op jit(solution)/shard_map/ppermute | solution.py:16
  273.8 7.0 %collective-permute-start.27 = (f32[24,8,144]{2,1,0:T(8,128)S(1)}, f32[24,8,144]{2,1,0:T(8,128)S(1)}, u32[]{:S(2)}, u32[]{:S(2)}) collective-permute-start(f32[24,8,144]{2,1,0:T(8,128)S(1)} %get-tuple-element.10), channel_id=1, source_target_pairs={{4,0},{8,4},{12,8},{16,12},{20,16},{24,20},{28,24},{32,28},{36,32}... | collective-permute-start | bytes 331784 | tf_op jit(solution)/shard_map/ppermute | solution.py:17
  281.1 5.6 %collective-permute-start.28 = (f32[24,24,8]{2,1,0:T(8,128)S(1)}, f32[24,24,8]{2,1,0:T(8,128)S(1)}, u32[]{:S(2)}, u32[]{:S(2)}) collective-permute-start(f32[24,24,8]{2,1,0:T(8,128)S(1)} %get-tuple-element.17), channel_id=1, source_target_pairs={{0,1},{1,2},{2,3},{4,5},{5,6},{6,7},{8,9},{9,10},{10,11},{12,13},{... | collective-permute-start | bytes 55304 | tf_op jit(solution)/shard_map/ppermute | solution.py:16
  283.0 7.7 %collective-permute-start.29 = (f32[24,24,8]{2,1,0:T(8,128)S(1)}, f32[24,24,8]{2,1,0:T(8,128)S(1)}, u32[]{:S(2)}, u32[]{:S(2)}) collective-permute-start(f32[24,24,8]{2,1,0:T(8,128)S(1)} %get-tuple-element.18), channel_id=1, source_target_pairs={{1,0},{2,1},{3,2},{5,4},{6,5},{7,6},{9,8},{10,9},{11,10},{13,12},{... | collective-permute-start | bytes 55304 | tf_op jit(solution)/shard_map/ppermute | solution.py:17
where the time goes:
time: 293 us; the launch traced here: 292 us
  starting transfers between devices  132 us (45%)
  waiting for transfers between devices  127 us (43%)
  matrix products  22.6 us (8%)
  local copies, waits for them, and re-layouts  5.66 us (2%)
  other arithmetic  4.06 us (1%)
    ppermute x15, waiting for transfers between devices, padded_2(): after = lax.ppermute(leading, axis, down)  101 us
    ppermute x15, starting transfers between devices, padded_2(): before = lax.ppermute(last, axis, up)  100 us
    ppermute x15, starting transfers between devices, padded_2(): after = lax.ppermute(leading, axis, down)  31.6 us
    ppermute x15, waiting for transfers between devices, padded_2(): before = lax.ppermute(last, axis, up)  26.1 us
  transfers between devices with their start and end apart: 30, of which 26 were waited for; matrix products, arithmetic and copies ran while one was open for 1% of the time, Pallas kernels for 0%

commit v1 on v0

v1 whole, which is shorter than its diff:
```python
import jax
import jax.numpy as jnp
from jax import lax
from jax.experimental import pallas as pl
from jax.experimental.pallas import tpu as pltpu
from jax.sharding import PartitionSpec as P

MESH = pl.DeviceIdType.MESH
F32 = jnp.float32
BF16 = jnp.bfloat16
DIRS = [(dy, dz) for dy in (-1, 0, 1) for dz in (-1, 0, 1) if (dy, dz) != (0, 0)]
PARTS8 = ((0, 2), (2, 2), (4, 2), (6, 2))
PARTS17 = ((0, 6), (6, 4), (10, 4), (14, 3))


def split(x):
    hi = x.astype(BF16)
    return hi, (x - hi.astype(F32)).astype(BF16)


def mm(a, b):
    return lax.dot_general(a, b, (((1,), (0,)), ((), ())), preferred_element_type=F32)


def roll(x, shift):
    return pltpu.roll(x, shift % x.shape[-1], x.ndim - 1)


def kernel(sizes, f, rea, bx, by, bz, ex, ey, ez, out,
           E0, E1, RE0, RE1, T0, T1, U0, U1, V0, V1, inv, S,
           wz32, wxy32, wzf, wzb, wxf, wxb, wyf, wyb,
           pfA, pfB, pr, pm, pv, pl2H, pl2O,
           rfA, rfB, rr, rmf, rmc, rmy, rvz, rvc, R, RR,
           r2f, r2c, r2y, q2f, q2c, q2y, XL, XR, X2, RB8a, RB17, RB8b,
           ssem, rsem):
    n_gx, n_gy, n_gz = sizes
    gx, gy, gz = (lax.axis_index(a) for a in ("gx", "gy", "gz"))
    relay = n_gx == 8
    mid = n_gx // 2 - 1
    has_y = {-1: gy > 0, 0: gy >= 0, 1: gy < n_gy - 1}
    has_z = {-1: gz > 0, 0: gz >= 0, 1: gz < n_gz - 1}
    has_x = {-1: gx > 0, 1: gx < n_gx - 1}
    has = {d: has_y[d[0]] & has_z[d[1]] for d in DIRS}
    lane = lax.broadcasted_iota(jnp.int32, (8, 128), 1)
    sub = lax.broadcasted_iota(jnp.int32, (8, 128), 0)

    def lanes(rows):
        return lax.broadcasted_iota(jnp.int32, (rows, 128), 1)

    counter = [0]

    def slots(n):
        counter[0] += n
        return counter[0] - n

    def copy(k, src, dst, dev):
        return pltpu.make_async_remote_copy(
            src_ref=src, dst_ref=dst, send_sem=ssem.at[k], recv_sem=rsem.at[k],
            device_id=dev, device_id_type=MESH)

    class YZ:
        def __init__(self, items):
            self.items = {d: items(d) for d in DIRS}
            self.k = {d: slots(len(self.items[d])) for d in DIRS}

        def each(self, d, along):
            dev = (gx, gy + d[0], gz + d[1])
            for j, (src, dst) in enumerate(self.items[along]):
                yield copy(self.k[along] + j, src, dst, dev)

        def start(self):
            for d in DIRS:
                @pl.when(has[d])
                def _():
                    for c in self.each(d, d):
                        c.start()

        def wait(self):
            for d in DIRS:
                @pl.when(has[d])
                def _():
                    for c in self.each(d, (-d[0], -d[1])):
                        c.wait_recv()
                    for c in self.each(d, d):
                        c.wait_send()

    class XX:
        def __init__(self, srcs, dsts, parts=None, rb=None):
            self.srcs, self.dsts, self.rb = srcs, dsts, rb
            self.parts = parts if relay else None
            self.k = {s: slots(1) for s in (-1, 1)}
            if self.parts:
                self.kr = slots(1)
                self.kp = {s: slots(4) for s in (-1, 1)}

        def end(self, s):
            return mid if s == 1 else mid + 1

        def via(self, s, j):
            return self.end(s) - s * j

        def whole(self, s):
            return copy(self.k[s], self.srcs[s], self.dsts[s], (gx + s, gy, gz))

        def part(self, s, j, src=None):
            lo, n = self.parts[j]
            src = self.srcs[s].at[pl.ds(lo, n)] if src is None else src
            return copy(self.kp[s] + j, src, self.dsts[s].at[pl.ds(lo, n)], (self.end(s) + s, gy, gz))

        def leg(self, s, j):
            lo, n = self.parts[j]
            return copy(self.kr, self.srcs[s].at[pl.ds(lo, n)], self.rb.at[pl.ds(0, n)], (self.via(s, j), gy, gz))

        def leg_send(self, s, j):
            lo, n = self.parts[j]
            return pltpu.make_async_remote_copy(
                src_ref=self.srcs[s].at[pl.ds(lo, n)], dst_ref=self.rb.at[pl.ds(0, n)],
                send_sem=ssem.at[self.kp[s] + j], recv_sem=rsem.at[self.kr],
                device_id=(self.via(s, j), gy, gz), device_id_type=MESH)

        def start(self):
            for s in (1, -1):
                if self.parts:
                    @pl.when(has_x[s] & (gx != self.end(s)))
                    def _():
                        self.whole(s).start()

                    @pl.when(gx == self.end(s))
                    def _():
                        for j in (1, 2, 3):
                            self.leg_send(s, j).start()
                        self.part(s, 0).start()
                else:
                    @pl.when(has_x[s])
                    def _():
                        self.whole(s).start()

        def forward(self):
            if self.parts:
                for s in (1, -1):
                    for j in (1, 2, 3):
                        @pl.when(gx == self.via(s, j))
                        def _():
                            self.leg(s, j).wait_recv()
                            self.part(s, j, self.rb.at[pl.ds(0, self.parts[j][1])]).start()

        def wait(self):
            for s in (1, -1):
                if self.parts:
                    @pl.when(has_x[-s] & (gx != self.end(s) + s))
                    def _():
                        self.whole(s).wait_recv()

                    @pl.when(gx == self.end(s) + s)
                    def _():
                        for j in range(4):
                            self.part(s, j).wait_recv()

                    @pl.when(has_x[s] & (gx != self.end(s)))
                    def _():
                        self.whole(s).wait_send()

                    @pl.when(gx == self.end(s))
                    def _():
                        for j in (1, 2, 3):
                            self.leg_send(s, j).wait_send()
                        self.part(s, 0).wait_send()

                    for j in (1, 2, 3):
                        @pl.when(gx == self.via(s, j))
                        def _():
                            self.part(s, j, self.rb.at[pl.ds(0, self.parts[j][1])]).wait_send()
                else:
                    @pl.when(has_x[-s])
                    def _():
                        self.whole(s).wait_recv()

                    @pl.when(has_x[s])
                    def _():
                        self.whole(s).wait_send()

    barrier = pltpu.get_barrier_semaphore()
    expect = jnp.int32(0)
    for d in DIRS:
        @pl.when(has[d])
        def _():
            pl.semaphore_signal(barrier, inc=1, device_id=(gx, gy + d[0], gz + d[1]), device_id_type=MESH)
        expect = expect + has[d].astype(jnp.int32)
    for s in (-1, 1):
        @pl.when(has_x[s])
        def _():
            pl.semaphore_signal(barrier, inc=1, device_id=(gx + s, gy, gz), device_id_type=MESH)
        expect = expect + has_x[s].astype(jnp.int32)
    if relay:
        pairs = []
        for s in (-1, 1):
            e = mid if s == 1 else mid + 1
            pairs += [(e, e - s * j) for j in (2, 3)] + [(e - s * j, e + s) for j in (1, 2, 3)]
        for a, b in pairs:
            for me, other in ((a, b), (b, a)):
                @pl.when(gx == me)
                def _():
                    pl.semaphore_signal(barrier, inc=1, device_id=(jnp.int32(other), gy, gz), device_id_type=MESH)
                expect = expect + (gx == me).astype(jnp.int32)

    def edge(x, width):
        ln = lanes(x.shape[0])
        return jnp.where((ln < width) | (ln >= 128 - width), x, 0.0)

    def pack(dst, load, groups, per, stride, masked):
        def body(g, c):
            acc = None
            for i in range(per):
                x = load(g * per + i)
                if masked:
                    x = edge(x, stride // 2)
                if i:
                    x = roll(x, stride * i)
                acc = x if acc is None else acc + x
            dst[g] = acc
            return c
        lax.fori_loop(0, groups, body, 0)

    def low_part(rows, stride):
        ln = lanes(rows)
        return (lax.rem(ln, stride) < stride // 2) & (ln < 128 - stride // 2 if stride == 18 else ln >= 0)

    def zero_missing(buf_of):
        for d in DIRS:
            bufs = buf_of(d)
            if bufs:
                @pl.when(jnp.logical_not(has[(-d[0], -d[1])]))
                def _():
                    for b in bufs:
                        b[...] = jnp.zeros(b.shape, F32)

    def halo_items(src, x0, nx, dst, packed, recv):
        rows = {0: (0, 24, 0), 1: (16, 8, 32), -1: (0, 8, 24)}

        def items(d):
            s, n, t = rows[d[0]]
            if d[1] == 0:
                return [(src.at[pl.ds(x0 if src is not f and src is not rea else 0, nx), pl.ds(s, n)],
                         dst.at[pl.ds(x0, nx), pl.ds(t, n)])]
            return [(packed.at[:, pl.ds(s, n)], recv.at[0 if d[1] == 1 else 1, :, pl.ds(t, n)])]
        return items

    def fold_items(a0s, packed, recv_f, recv_c, recv_y):
        rows = {1: 24, -1: 32}

        def items(d):
            z = 0 if d[1] == 1 else 1
            y = 0 if d[0] == 1 else 1
            if d[1] == 0:
                return [(U0.at[pl.ds(a, n), pl.ds(rows[d[0]], 8)], recv_y.at[y, pl.ds(t, n)]) for a, n, t in a0s]
            if d[0] == 0:
                return [(packed.at[:, pl.ds(0, 24)], recv_f.at[z])]
            return [(packed.at[:, pl.ds(rows[d[0]], 8)], recv_c.at[y, z])]
        return items

    def layer_items(d):
        z = 0 if d[1] == 1 else 1
        y = 0 if d[0] == 1 else 1
        if d[1] == 0:
            s, t = ((16, 40), (0, 24))[y]
            return [(V0.at[:, pl.ds(s, 8)], V0.at[:, pl.ds(t, 8)]), (R.at[y], RR.at[y])]
        if d[0] == 0:
            return [(pv, rvz.at[z])]
        return [(pv.at[:, pl.ds(8 if y == 0 else 0, 16)], rvc.at[y, z])]

    xf = XX({1: f.at[pl.ds(16, 8)], -1: f.at[pl.ds(0, 8)]},
            {1: E0.at[pl.ds(32, 8), pl.ds(0, 24)], -1: E0.at[pl.ds(24, 8), pl.ds(0, 24)]}, PARTS8, RB8a)
    xr = XX({1: rea.at[pl.ds(16, 8)], -1: rea.at[pl.ds(0, 8)]},
            {1: RE0.at[pl.ds(32, 8), pl.ds(0, 24)], -1: RE0.at[pl.ds(24, 8), pl.ds(0, 24)]})
    fA = YZ(halo_items(f, 0, 24, E0, pfA, rfA))
    fB = YZ(halo_items(E0, 24, 16, E0, pfB, rfB))
    rA = YZ(halo_items(RE0, 0, 40, RE0, pr, rr))
    m1 = YZ(fold_items([(0, 40, 0)], pm, rmf, rmc, rmy))
    m2 = XX({1: S.at[pl.ds(23, 17)], -1: S.at[pl.ds(0, 17)]}, {1: XL, -1: XR}, PARTS17, RB17)
    m3 = YZ(layer_items)
    l2H = YZ(fold_items([(0, 8, 0), (32, 8, 8)], pl2H, r2f, r2c, r2y))
    l2O = YZ(fold_items([(8, 24, 0)], pl2O, q2f, q2c, q2y))
    x2 = XX({1: S.at[pl.ds(32, 8)], -1: S.at[pl.ds(0, 8)]}, {1: X2.at[0], -1: X2.at[1]}, PARTS8, RB8b)

    E0[pl.ds(0, 24), pl.ds(0, 24)] = f[...]
    pack(pfA, lambda i: f[i], 3, 8, 16, True)

    wz32[...] = jnp.zeros((256, 256), F32)
    wz32[0:128, 0:144] = bz[8:136, :]
    wz32[128:136, 0:144] = bz[136:144, :]
    wz32[248:256, 0:144] = bz[0:8, :]
    for w, table in ((wzf, wz32[...]), (wzb, wz32[...].T)):
        hi, lo = split(table)
        w[0:256] = hi
        w[256:512] = hi
        w[512:768] = lo

    def blocks(w, m):
        wxy32[...] = jnp.zeros((80, 256), F32)
        hi, lo = split(m)
        hi, lo = hi.astype(F32), lo.astype(F32)
        for j, part in enumerate((hi, hi, lo)):
            wxy32[0:40, 80 * j:80 * j + 40] = part
            wxy32[40:80, 80 * j + 40:80 * j + 80] = part
        w[...] = wxy32[...].astype(BF16)

    x_nat, y_nat = bx[...], by[...]
    x_circ = jnp.concatenate([x_nat[8:40], x_nat[0:8]], axis=0)
    y_circ = jnp.concatenate([y_nat[8:40], y_nat[0:8]], axis=0)
    blocks(wxf, x_circ.T)
    blocks(wxb, x_nat)
    blocks(wyf, y_circ.T)
    blocks(wyb, y_circ)

    column = lax.broadcasted_iota(jnp.int32, (40, 128), 0)
    exc = lax.fori_loop(0, 40, lambda p, c: jnp.where(column == p, ex[p], c), jnp.zeros((40, 128), F32))
    ez0 = jnp.broadcast_to(ez[:, 0:128], (40, 128))
    ez1 = jnp.broadcast_to(ez[:, 128:256], (40, 128))

    def table(q, c):
        base = exc + ey[q]
        inv[0, q] = 1.0 / (base + ez0)
        inv[1, q] = 1.0 / (base + ez1)
        return c
    lax.fori_loop(0, 40, table, 0)

    def zrows(b, x0, nx, t):
        for i in range(nx // 8):
            b[pl.ds(x0 + 8 * i, 8), pl.ds(t, 8)] = jnp.zeros((8, 8, 128), F32)

    for s, x0 in ((-1, 32), (1, 24)):
        @pl.when(jnp.logical_not(has_x[s]))
        def _():
            for b in (E0, RE0):
                b[pl.ds(x0, 8), pl.ds(0, 24)] = jnp.zeros((8, 24, 128), F32)
            (XL if s == -1 else XR)[...] = jnp.zeros((17, 24, 128), F32)
            X2[0 if s == -1 else 1] = jnp.zeros((8, 24, 128), F32)
    for s, t, tv in ((-1, 32, 40), (1, 24, 24)):
        @pl.when(jnp.logical_not(has_y[s]))
        def _():
            for b in (E0, RE0):
                zrows(b, 0, 40, t)
            zrows(V0, 0, 40, tv)
            V0[pl.ds(40, 2), pl.ds(tv, 8)] = jnp.zeros((2, 8, 128), F32)
            RR[0 if s == -1 else 1] = jnp.zeros((48, 128), F32)
            for b in (rmy, r2y, q2y):
                b[0 if s == -1 else 1] = jnp.zeros(b.shape[1:], F32)

    def missing(d):
        z = 0 if d[1] == 1 else 1
        y = 0 if d[0] == 1 else 1
        t, n = {0: (0, 24), 1: (32, 8), -1: (24, 8)}[d[0]]
        if d[1] == 0:
            return []
        out_ = [b.at[z, :, pl.ds(t, n)] for b in (rfA, rfB, rr)]
        if d[0] == 0:
            return out_ + [b.at[z] for b in (rmf, r2f, q2f, rvz)]
        return out_ + [b.at[y, z] for b in (rmc, r2c, q2c, rvc)]
    zero_missing(missing)

    pl.semaphore_wait(barrier, expect)

    def unpack_halo(recv, g0, groups, dst1, x0):
        def body(g, c):
            both = jnp.where(low_part(40, 16), recv[1, g], recv[0, g])
            for i in range(8):
                dst1[x0 + g * 8 + i] = edge(roll(both, -16 * i), 8)
            return c
        lax.fori_loop(g0, g0 + groups, body, 0)

    def cat3(x0, x1):
        h0, l0 = split(x0)
        h1, l1 = split(x1)
        return jnp.concatenate([h0, h1, l0, l1, h0, h1], axis=1)

    def stack3(x):
        hi, lo = split(x)
        return jnp.concatenate([hi, lo, hi], axis=0)

    def forward_chunk(c, _):
        x0 = E0[pl.ds(8 * c, 8)].reshape(320, 128)
        x1 = E1[pl.ds(8 * c, 8)].reshape(320, 128)
        z = mm(cat3(x0, x1), wzf[...])
        for i in range(4):
            y = mm(wyf[:, 0:240], stack3(z[80 * i:80 * i + 80]))
            T0[pl.ds(320 * c + 80 * i, 80), :] = y[:, 0:128]
            T1[pl.ds(320 * c + 80 * i, 80), :] = y[:, 128:256]
        return _

    def middle(j, _):
        parts = []
        for i in range(2):
            q = 2 * j + i
            parts.append(jnp.concatenate([T0[pl.ds(q, 40, stride=40), :], T1[pl.ds(q, 40, stride=40), :]], axis=1))
        m = mm(wxf[:, 0:240], stack3(jnp.concatenate(parts, axis=0)))
        scale = jnp.concatenate([
            jnp.concatenate([inv[0, 2 * j + i], inv[1, 2 * j + i]], axis=1) for i in range(2)], axis=0)
        m = mm(wxb[:, 0:240], stack3(m * scale))
        for i in range(2):
            q = 2 * j + i
            T0[pl.ds(q, 40, stride=40), :] = m[40 * i:40 * i + 40, 0:128]
            T1[pl.ds(q, 40, stride=40), :] = m[40 * i:40 * i + 40, 128:256]
        return _

    def back_chunk(c, _):
        parts = []
        for i in range(4):
            x = jnp.concatenate([T0[pl.ds(320 * c + 80 * i, 80), :], T1[pl.ds(320 * c + 80 * i, 80), :]], axis=1)
            parts.append(mm(wyb[:, 0:240], stack3(x)))
        y = jnp.concatenate(parts, axis=0)
        z = mm(cat3(y[:, 0:128], y[:, 128:256]), wzb[...])
        U0[pl.ds(8 * c, 8)] = z[:, 0:128].reshape(8, 40, 128)
        U1[pl.ds(8 * c, 8)] = z[:, 128:256].reshape(8, 40, 128)
        return _

    def fold(a0, g0, groups, y0, recv_f, recv_c, recv_y):
        def body(g, c):
            both = jnp.where(low_part(24, 16), recv_f[0, g], recv_f[1, g])
            low = low_part(8, 16)
            first = jnp.where(low, recv_c[0, 0, g], recv_c[0, 1, g])
            last = jnp.where(low, recv_c[1, 0, g], recv_c[1, 1, g])
            both = both + jnp.concatenate([first, jnp.zeros((8, 128), F32), last], axis=0)
            for i in range(8):
                a = a0 + 8 * (g - g0) + i
                t = y0 + 8 * (g - g0) + i
                zpart = edge(roll(both, -16 * i), 8)
                ypart = jnp.concatenate([recv_y[0, t], jnp.zeros((8, 128), F32), recv_y[1, t]], axis=0)
                S[a] = U0[a, pl.ds(0, 24)] + (zpart + ypart)
            return c
        lax.fori_loop(g0, g0 + groups, body, 0)

    xf.start()
    fA.start()
    xf.forward()
    fA.wait()
    unpack_halo(rfA, 0, 3, E1, 0)
    lax.fori_loop(0, 3, forward_chunk, 0)
    xf.wait()
    pack(pfB, lambda i: E0[24 + i, pl.ds(0, 24)], 2, 8, 16, True)
    fB.start()
    xr.start()
    fB.wait()
    unpack_halo(rfB, 0, 2, E1, 24)
    lax.fori_loop(3, 5, forward_chunk, 0)
    lax.fori_loop(0, 20, middle, 0)
    lax.fori_loop(0, 5, back_chunk, 0)
    pack(pm, lambda i: U1[i], 5, 8, 16, False)
    m1.start()
    m1.wait()
    fold(0, 0, 5, 0, rmf, rmc, rmy)
    m2.start()
    m2.forward()

    RE0[pl.ds(0, 24), pl.ds(0, 24)] = rea[...]
    xr.wait()
    pack(pr, lambda i: RE0[i, pl.ds(0, 24)], 5, 8, 16, True)
    rA.start()
    rA.wait()
    unpack_halo(rr, 0, 5, RE1, 0)
    m2.wait()

    def build_a(i, c):
        V0[i + 1, pl.ds(0, 24)] = S[i] + XL[i + 1]
        V0[i + 25, pl.ds(0, 24)] = S[i + 24] + XR[i]
        return c
    lax.fori_loop(0, 16, build_a, 0)
    for i in range(8):
        V0[17 + i, pl.ds(0, 24)] = S[16 + i]
    V0[0, pl.ds(0, 24)] = XL[0]
    V0[41, pl.ds(0, 24)] = XR[16]
    for s, v in ((-1, 0), (1, 33)):
        @pl.when(jnp.logical_not(has_x[s]))
        def _():
            V0[pl.ds(v, 9), pl.ds(0, 24)] = jnp.zeros((9, 24, 128), F32)
    R[...] = jnp.zeros((2, 48, 128), F32)
    for i in range(42):
        R[0, i:i + 1, :] = V0[i, 15:16, :]
        R[1, i:i + 1, :] = V0[i, 8:9, :]
    pack(pv, lambda i: V0[i, pl.ds(0, 24)], 6, 7, 18, True)
    m3.start()
    m3.wait()
    for i in range(42):
        V0[i, 39:40, :] = RR[0, i:i + 1, :]
        V0[i, 32:33, :] = RR[1, i:i + 1, :]

    def unpack_layer(g, c):
        face = jnp.where(low_part(24, 18), rvz[1, g], rvz[0, g])
        low = low_part(16, 18)
        lo_y = jnp.where(low, rvc[0, 1, g], rvc[0, 0, g])
        hi_y = jnp.where(low, rvc[1, 1, g], rvc[1, 0, g])
        between = jnp.where(sub == 0, hi_y[8:16], lo_y[0:8])
        both = jnp.concatenate([face, hi_y[0:8], between, lo_y[8:16]], axis=0)
        for i in range(7):
            V1[g * 7 + i] = edge(roll(both, -18 * i), 9)
        return c
    lax.fori_loop(0, 6, unpack_layer, 0)

    row = lax.broadcasted_iota(jnp.int32, (40, 128), 0)
    ln = lanes(40)
    inside_y = jnp.logical_not(((row >= 24) & (row < 32) & jnp.logical_not(has_y[1]))
                               | ((row >= 32) & jnp.logical_not(has_y[-1])))
    mask0 = jnp.where(inside_y, 1.0, 0.0)
    mask1 = jnp.where(inside_y & (((ln < 8) & has_z[1]) | ((ln >= 120) & has_z[-1])), 1.0, 0.0)
    ln48 = lanes(48)

    def shifts(v0, v1):
        p0, p1 = roll(v0, -1), roll(v1, -1)
        n0, n1 = roll(v0, 1), roll(v1, 1)
        top, bottom = ln48 == 127, ln48 == 0
        z0 = jnp.where(top, p1, p0) + jnp.where(bottom, n1, n0)
        z1 = jnp.where(top, p0, p1) + jnp.where(bottom, n0, n1)
        return z0 + 2.0 * v0, z1 + 2.0 * v1

    def sum_y(x):
        return pltpu.roll(x, 47, 0) + pltpu.roll(x, 1, 0)

    def level(v):
        v0, v1 = V0[v], V1[v]
        a0, a1 = shifts(v0, v1)
        b0, b1 = sum_y(a0) + 2.0 * a0, sum_y(a1) + 2.0 * a1
        return a0, a1, b0, b1

    def ext(x):
        return jnp.concatenate([x[0:32], x[40:48]], axis=0)

    def stencil(a, c):
        bm0, bm1, a0, a1, b0, b1 = c
        na0, na1, nb0, nb1 = level(a + 2)
        x = jnp.where(a < 8, a + 32, a - 8)
        inside = jnp.where(((a < 8) & jnp.logical_not(has_x[-1])) | ((a >= 32) & jnp.logical_not(has_x[1])), 0.0, 1.0)
        for V, E, RE, m, bm, aa, b, nb in ((V0, E0, RE0, mask0, bm0, a0, b0, nb0), (V1, E1, RE1, mask1, bm1, a1, b1, nb1)):
            v = V[a + 1]
            axis = V[a] + V[a + 2] + sum_y(v) + (aa - 2.0 * v)
            k = 5.5 * v - 0.25 * axis - 0.0625 * (bm + nb + 2.0 * b)
            E[x] = (E[x] - (RE[x] * ext(v) + ext(k))) * (m * inside)
        return b0, b1, na0, na1, nb0, nb1

    l0 = level(0)
    l1 = level(1)
    lax.fori_loop(0, 40, stencil, (l0[2], l0[3], l1[0], l1[1], l1[2], l1[3]))

    lax.fori_loop(0, 5, forward_chunk, 0)
    lax.fori_loop(0, 20, middle, 0)
    back_chunk(0, 0)
    back_chunk(4, 0)
    pack(pl2H, lambda i: U1[jnp.where(i < 8, i, i + 24)], 2, 8, 16, False)
    l2H.start()
    lax.fori_loop(1, 4, back_chunk, 0)
    pack(pl2O, lambda i: U1[i + 8], 3, 8, 16, False)
    l2O.start()
    l2H.wait()
    fold(0, 0, 1, 0, r2f, r2c, r2y)
    fold(32, 1, 1, 8, r2f, r2c, r2y)
    x2.start()
    x2.forward()
    l2O.wait()
    fold(8, 0, 3, 0, q2f, q2c, q2y)
    x2.wait()

    def finish(i, c):
        out[i] = V0[i + 9, pl.ds(0, 24)] + (S[i + 8] + X2[0, i])
        out[i + 8] = V0[i + 17, pl.ds(0, 24)] + S[i + 16]
        out[i + 16] = V0[i + 25, pl.ds(0, 24)] + (S[i + 24] + X2[1, i])
        return c
    lax.fori_loop(0, 8, finish, 0)


def solution(mesh):
    sizes = tuple(mesh.shape[a] for a in ("gx", "gy", "gz"))

    def local(right_side, reaction, basis_x, basis_y, basis_z, eigen_x, eigen_y, eigen_z):
        def vm(*shape, dtype=F32):
            return pltpu.VMEM(shape, dtype)
        scratch = [vm(40, 40, 128), vm(40, 40, 128), vm(40, 40, 128), vm(40, 40, 128),
                   vm(1600, 128), vm(1600, 128), vm(40, 40, 128), vm(40, 40, 128),
                   vm(42, 48, 128), vm(42, 48, 128), vm(2, 40, 40, 128), vm(40, 24, 128),
                   vm(256, 256), vm(80, 256), vm(768, 256, dtype=BF16), vm(768, 256, dtype=BF16)]
        scratch += [vm(80, 256, dtype=BF16)] * 4
        scratch += [vm(3, 24, 128), vm(2, 24, 128), vm(5, 24, 128), vm(5, 40, 128), vm(6, 24, 128),
                    vm(2, 40, 128), vm(3, 40, 128)]
        scratch += [vm(2, 3, 40, 128), vm(2, 2, 40, 128), vm(2, 5, 40, 128),
                    vm(2, 5, 24, 128), vm(2, 2, 5, 8, 128), vm(2, 40, 8, 128),
                    vm(2, 6, 24, 128), vm(2, 2, 6, 16, 128), vm(2, 48, 128), vm(2, 48, 128),
                    vm(2, 2, 24, 128), vm(2, 2, 2, 8, 128), vm(2, 16, 8, 128),
                    vm(2, 3, 24, 128), vm(2, 2, 3, 8, 128), vm(2, 24, 8, 128),
                    vm(17, 24, 128), vm(17, 24, 128), vm(2, 8, 24, 128),
                    vm(2, 24, 128), vm(4, 24, 128), vm(2, 24, 128),
                    pltpu.SemaphoreType.DMA((120,)), pltpu.SemaphoreType.DMA((120,))]
        vmem = pl.BlockSpec(memory_space=pltpu.VMEM)
        smem = pl.BlockSpec(memory_space=pltpu.SMEM)
        row_z = jnp.pad(eigen_z, (0, 112), constant_values=1.0).reshape(1, 256)

        def body(*refs):
            kernel(sizes, *refs)

        return pl.pallas_call(
            body,
            out_shape=jax.ShapeDtypeStruct((24, 24, 128), F32),
            in_specs=[vmem] * 5 + [smem, smem, vmem],
            out_specs=vmem,
            scratch_shapes=scratch,
            compiler_params=pltpu.CompilerParams(
                collective_id=0, has_side_effects=True, vmem_limit_bytes=40 * 1024 * 1024),
            cost_estimate=pl.CostEstimate(flops=1200000000, bytes_accessed=2000000, transcendentals=0),
        )(right_side, reaction, basis_x, basis_y, basis_z, eigen_x, eigen_y, row_z)

    return jax.shard_map(
        local,
        mesh=mesh,
        in_specs=(P("gx", "gy", "gz"), P("gx", "gy", "gz"), P(), P(), P(), P(), P(), P()),
        out_specs=P("gx", "gy", "gz"),
        check_vma=False,
    )
```

time: 293 us -> 108 us (0.37)
  starting transfers between devices: 132 us -> 0 us
  waiting for transfers between devices: 127 us -> 0 us
  Pallas kernels: 0 us -> 99.7 us
  matrix products: 22.6 us -> 0 us
  other arithmetic: 4.06 us -> 0 us
    ppermute x30 -> x0, starting transfers between devices: 132 us -> none  [the longest x15 100 us: padded_2(): before = lax.ppermute(last, axis, up)]
    ppermute x30 -> x0, waiting for transfers between devices: 127 us -> none  [the longest x15 101 us: padded_2(): after = lax.ppermute(leading, axis, down)]
    pallas_call x0 -> x1, Pallas kernels: none -> 99.7 us  [local(): pl.pallas_call(body, out_shape=jax.ShapeDtypeStruct((24, 24, 128), F32),...]
    dot_general x12 -> x0, matrix products: 22.6 us -> none  [the longest x2 4.22 us: local_solve(): back = jnp.einsum('ap,pqs->aqs', basis_x, modes, precision=highest)]
    unnamed x20 -> x15, local copies, waits for them, and re-layouts: 1.55 us -> 5.67 us
  transfers between devices with their start and end apart: 30 -> 0, of which waited for: 26 -> 0; matrix products, arithmetic and copies ran while one was open for 1% -> 0% of each run, Pallas kernels for 0% -> 0%
where the time goes in v1:
time: 108 us; the launch traced here: 106 us
  Pallas kernels  99.7 us (92%)
  local copies, waits for them, and re-layouts  6.35 us (6%)
    pallas_call x1, Pallas kernels, local(): pl.pallas_call(body, out_shape=jax.ShapeDtypeStruct((24, 24, 128), F32),...  99.7 us
    unnamed x15, local copies, waits for them, and re-layouts  5.67 us

profile of v1, /device:TPU:7, one launch (start us, length us, event | category | flops | bytes accessed | tf_op | source)
XLA Modules:
  0.0 106.0 jit_solution(12884539554536593730)
XLA Ops:
  0.0 0.7 pad.4
  0.7 0.0 copy-start.5
  0.7 0.0 copy-start.6
  0.7 0.7 copy-done.5
  1.3 0.0 copy-done.6
  1.4 0.0 copy-start
  1.4 1.0 copy-done
  2.3 0.0 copy-start.1
  2.3 1.0 copy-done.1
  3.3 0.0 copy-start.2
  3.3 0.9 copy-done.2
  4.2 0.0 copy-start.3
  4.2 0.7 copy-done.3
  4.9 0.0 copy-start.4
  4.9 0.7 copy-done.4
  5.6 99.7 %shard_map.82 = f32[24,24,128]{2,1,0:T(8,128)S(1)} custom-call(f32[24,24,128]{2,1,0:T(8,128)S(1)} %copy-done, f32[24,24,128]{2,1,0:T(8,128)S(1)} %copy-done.1, f32[40,40]{1,0:T(8,128)S(1)} %copy-done.3, f32[40,40]{1,0:T(8,128)S(1)} %copy-done.4, f32[144,144]{1,0:T(8,128)S(1)} %copy-done.2, f32[40]{0:T(128)S(1)} %copy-done.5, f32[40]{0:T(128)S(1)} %copy-done.6, ...), custom_call_target="tpu_custom_call" | custom-call | flops 1200000000 | bytes 2000000 | tf_op jit(solution)/shard_map/pallas_call | solution.py:596
  105.3 0.7 copy.10
Async XLA Ops:
  0.7 0.7 copy-start.5
  0.7 0.7 copy-start.6
  1.4 1.0 copy-start
  2.3 1.0 copy-start.1
  3.3 0.9 copy-start.2
  4.2 0.7 copy-start.3
  4.9 0.7 copy-start.4

commit v2 on v1

--- a/solution.py
+++ b/solution.py
@@ -8,6 +8,7 @@
 MESH = pl.DeviceIdType.MESH
 F32 = jnp.float32
 BF16 = jnp.bfloat16
+UL, US, UM, UF, UB = 3, 4, 10, True, True
 DIRS = [(dy, dz) for dy in (-1, 0, 1) for dz in (-1, 0, 1) if (dy, dz) != (0, 0)]
 PARTS8 = ((0, 2), (2, 2), (4, 2), (6, 2))
 PARTS17 = ((0, 6), (6, 4), (10, 4), (14, 3))
@@ -26,13 +27,14 @@
     return pltpu.roll(x, shift % x.shape[-1], x.ndim - 1)
 
 
-def kernel(sizes, f, rea, bx, by, bz, ex, ey, ez, out,
+def kernel(sizes, f_hbm, rea_hbm, bx_hbm, by_hbm, bz_hbm, ex, ey, ez, out,
+           f, rea, bx, by, bz,
            E0, E1, RE0, RE1, T0, T1, U0, U1, V0, V1, inv, S,
-           wz32, wxy32, wzf, wzb, wxf, wxb, wyf, wyb,
+           A0, A1, wz32, wxy32, wzf, wzb, wxf, wxb, wyf, wyb,
            pfA, pfB, pr, pm, pv, pl2H, pl2O,
            rfA, rfB, rr, rmf, rmc, rmy, rvz, rvc, R, RR,
            r2f, r2c, r2y, q2f, q2c, q2y, XL, XR, X2, RB8a, RB17, RB8b,
-           ssem, rsem):
+           ssem, rsem, lsem):
     n_gx, n_gy, n_gz = sizes
     gx, gy, gz = (lax.axis_index(a) for a in ("gx", "gy", "gz"))
     relay = n_gx == 8
@@ -203,6 +205,13 @@
                     pl.semaphore_signal(barrier, inc=1, device_id=(jnp.int32(other), gy, gz), device_id_type=MESH)
                 expect = expect + (gx == me).astype(jnp.int32)
 
+    loads = [pltpu.make_async_copy(a, b, lsem.at[i]) for i, (a, b) in enumerate(
+        ((f_hbm, f), (bz_hbm, bz), (bx_hbm, bx), (by_hbm, by), (rea_hbm, rea)))]
+    for c in loads:
+        c.start()
+    for c in loads[:4]:
+        c.wait()
+
     def edge(x, width):
         ln = lanes(x.shape[0])
         return jnp.where((ln < width) | (ln >= 128 - width), x, 0.0)
@@ -289,11 +298,18 @@
     wz32[0:128, 0:144] = bz[8:136, :]
     wz32[128:136, 0:144] = bz[136:144, :]
     wz32[248:256, 0:144] = bz[0:8, :]
-    for w, table in ((wzf, wz32[...]), (wzb, wz32[...].T)):
+    for w, table, turned in ((wzf, wz32[...], True), (wzb, wz32[...].T, False)):
         hi, lo = split(table)
-        w[0:256] = hi
-        w[256:512] = hi
-        w[512:768] = lo
+        w[0:128] = hi[0:128]
+        w[128:256] = hi[0:128]
+        w[256:384] = lo[0:128]
+        hi, lo = hi.astype(F32)[128:256], lo.astype(F32)[128:256]
+        if turned:
+            tail = jnp.concatenate([hi[0:8], hi[120:128], hi[0:8], lo[120:128], lo[0:8],
+                                    jnp.zeros((80, 256), F32), hi[120:128]], axis=0)
+        else:
+            tail = jnp.concatenate([hi[0:16], hi[0:16], lo[0:16], jnp.zeros((80, 256), F32)], axis=0)
+        w[384:512] = tail.astype(BF16)
 
     def blocks(w, m):
         wxy32[...] = jnp.zeros((80, 256), F32)
@@ -313,16 +329,20 @@
     blocks(wyb, y_circ)
 
     column = lax.broadcasted_iota(jnp.int32, (40, 128), 0)
-    exc = lax.fori_loop(0, 40, lambda p, c: jnp.where(column == p, ex[p], c), jnp.zeros((40, 128), F32))
-    ez0 = jnp.broadcast_to(ez[:, 0:128], (40, 128))
-    ez1 = jnp.broadcast_to(ez[:, 128:256], (40, 128))
+    exc = lax.fori_loop(0, 40, lambda p, c: jnp.where(column == p, ex[p], c), jnp.zeros((40, 128), F32), unroll=8)
+    ez0 = lax.fori_loop(0, 128, lambda p, c: jnp.where(lane == p, ez[p], c), jnp.ones((8, 128), F32), unroll=8)
+    ez1 = lax.fori_loop(0, 16, lambda p, c: jnp.where(lane == p, ez[p + 128], c), jnp.ones((8, 128), F32), unroll=8)
+    ez0, ez1 = (jnp.concatenate([e] * 5, axis=0) for e in (ez0, ez1))
 
     def table(q, c):
         base = exc + ey[q]
         inv[0, q] = 1.0 / (base + ez0)
         inv[1, q] = 1.0 / (base + ez1)
         return c
-    lax.fori_loop(0, 40, table, 0)
+    lax.fori_loop(0, 40, table, 0, unroll=2)
+
+    loads[4].wait()
+    RE0[pl.ds(0, 24), pl.ds(0, 24)] = rea[...]
 
     def zrows(b, x0, nx, t):
         for i in range(nx // 8):
@@ -370,8 +390,10 @@
 
     def cat3(x0, x1):
         h0, l0 = split(x0)
-        h1, l1 = split(x1)
-        return jnp.concatenate([h0, h1, l0, l1, h0, h1], axis=1)
+        h1 = x1.astype(BF16).astype(F32)
+        l1 = x1 - h1
+        tail = (h1 + roll(l1, 16) + roll(h1, 32)).astype(BF16)
+        return jnp.concatenate([h0, l0, h0, tail], axis=1)
 
     def stack3(x):
         hi, lo = split(x)
@@ -434,16 +456,16 @@
     xf.forward()
     fA.wait()
     unpack_halo(rfA, 0, 3, E1, 0)
-    lax.fori_loop(0, 3, forward_chunk, 0)
+    lax.fori_loop(0, 3, forward_chunk, 0, unroll=UF)
     xf.wait()
     pack(pfB, lambda i: E0[24 + i, pl.ds(0, 24)], 2, 8, 16, True)
     fB.start()
     xr.start()
     fB.wait()
     unpack_halo(rfB, 0, 2, E1, 24)
-    lax.fori_loop(3, 5, forward_chunk, 0)
-    lax.fori_loop(0, 20, middle, 0)
-    lax.fori_loop(0, 5, back_chunk, 0)
+    lax.fori_loop(3, 5, forward_chunk, 0, unroll=UF)
+    lax.fori_loop(0, 20, middle, 0, unroll=UM)
+    lax.fori_loop(0, 5, back_chunk, 0, unroll=UB)
     pack(pm, lambda i: U1[i], 5, 8, 16, False)
     m1.start()
     m1.wait()
@@ -451,7 +473,6 @@
     m2.start()
     m2.forward()
 
-    RE0[pl.ds(0, 24), pl.ds(0, 24)] = rea[...]
     xr.wait()
     pack(pr, lambda i: RE0[i, pl.ds(0, 24)], 5, 8, 16, True)
     rA.start()
@@ -511,41 +532,35 @@
         z1 = jnp.where(top, p0, p1) + jnp.where(bottom, n0, n1)
         return z0 + 2.0 * v0, z1 + 2.0 * v1
 
-    def sum_y(x):
-        return pltpu.roll(x, 47, 0) + pltpu.roll(x, 1, 0)
-
-    def level(v):
-        v0, v1 = V0[v], V1[v]
-        a0, a1 = shifts(v0, v1)
-        b0, b1 = sum_y(a0) + 2.0 * a0, sum_y(a1) + 2.0 * a1
-        return a0, a1, b0, b1
-
     def ext(x):
         return jnp.concatenate([x[0:32], x[40:48]], axis=0)
 
+    def level(v, c):
+        A0[v], A1[v] = shifts(V0[v], V1[v])
+        return c
+
     def stencil(a, c):
-        bm0, bm1, a0, a1, b0, b1 = c
-        na0, na1, nb0, nb1 = level(a + 2)
         x = jnp.where(a < 8, a + 32, a - 8)
         inside = jnp.where(((a < 8) & jnp.logical_not(has_x[-1])) | ((a >= 32) & jnp.logical_not(has_x[1])), 0.0, 1.0)
-        for V, E, RE, m, bm, aa, b, nb in ((V0, E0, RE0, mask0, bm0, a0, b0, nb0), (V1, E1, RE1, mask1, bm1, a1, b1, nb1)):
-            v = V[a + 1]
-            axis = V[a] + V[a + 2] + sum_y(v) + (aa - 2.0 * v)
-            k = 5.5 * v - 0.25 * axis - 0.0625 * (bm + nb + 2.0 * b)
+        for V, A, E, RE, m in ((V0, A0, E0, RE0, mask0), (V1, A1, E1, RE1, mask1)):
+            v, z = V[a + 1], A[a + 1]
+            total = A[a] + A[a + 2] + 2.0 * z
+            along = 0.25 * v + 0.0625 * total
+            k = 6.0 * v - 0.25 * (V[a] + V[a + 2] + z) - 0.125 * total
+            k = k - (pltpu.roll(along, 47, 0) + pltpu.roll(along, 1, 0))
             E[x] = (E[x] - (RE[x] * ext(v) + ext(k))) * (m * inside)
-        return b0, b1, na0, na1, nb0, nb1
-
-    l0 = level(0)
-    l1 = level(1)
-    lax.fori_loop(0, 40, stencil, (l0[2], l0[3], l1[0], l1[1], l1[2], l1[3]))
-
-    lax.fori_loop(0, 5, forward_chunk, 0)
-    lax.fori_loop(0, 20, middle, 0)
+        return c
+
+    lax.fori_loop(0, 42, level, 0, unroll=UL)
+    lax.fori_loop(0, 40, stencil, 0, unroll=US)
+
+    lax.fori_loop(0, 5, forward_chunk, 0, unroll=UF)
+    lax.fori_loop(0, 20, middle, 0, unroll=UM)
     back_chunk(0, 0)
     back_chunk(4, 0)
     pack(pl2H, lambda i: U1[jnp.where(i < 8, i, i + 24)], 2, 8, 16, False)
     l2H.start()
-    lax.fori_loop(1, 4, back_chunk, 0)
+    lax.fori_loop(1, 4, back_chunk, 0, unroll=UB)
     pack(pl2O, lambda i: U1[i + 8], 3, 8, 16, False)
     l2O.start()
     l2H.wait()
@@ -571,10 +586,12 @@
     def local(right_side, reaction, basis_x, basis_y, basis_z, eigen_x, eigen_y, eigen_z):
         def vm(*shape, dtype=F32):
             return pltpu.VMEM(shape, dtype)
-        scratch = [vm(40, 40, 128), vm(40, 40, 128), vm(40, 40, 128), vm(40, 40, 128),
+        scratch = [vm(24, 24, 128), vm(24, 24, 128), vm(40, 40), vm(40, 40), vm(144, 144)]
+        scratch += [vm(40, 40, 128), vm(40, 40, 128), vm(40, 40, 128), vm(40, 40, 128),
                    vm(1600, 128), vm(1600, 128), vm(40, 40, 128), vm(40, 40, 128),
                    vm(42, 48, 128), vm(42, 48, 128), vm(2, 40, 40, 128), vm(40, 24, 128),
-                   vm(256, 256), vm(80, 256), vm(768, 256, dtype=BF16), vm(768, 256, dtype=BF16)]
+                   vm(42, 48, 128), vm(42, 48, 128),
+                   vm(256, 256), vm(80, 256), vm(512, 256, dtype=BF16), vm(512, 256, dtype=BF16)]
         scratch += [vm(80, 256, dtype=BF16)] * 4
         scratch += [vm(3, 24, 128), vm(2, 24, 128), vm(5, 24, 128), vm(5, 40, 128), vm(6, 24, 128),
                     vm(2, 40, 128), vm(3, 40, 128)]
@@ -585,10 +602,10 @@
                     vm(2, 3, 24, 128), vm(2, 2, 3, 8, 128), vm(2, 24, 8, 128),
                     vm(17, 24, 128), vm(17, 24, 128), vm(2, 8, 24, 128),
                     vm(2, 24, 128), vm(4, 24, 128), vm(2, 24, 128),
-                    pltpu.SemaphoreType.DMA((120,)), pltpu.SemaphoreType.DMA((120,))]
+                    pltpu.SemaphoreType.DMA((120,)), pltpu.SemaphoreType.DMA((120,)), pltpu.SemaphoreType.DMA((5,))]
         vmem = pl.BlockSpec(memory_space=pltpu.VMEM)
         smem = pl.BlockSpec(memory_space=pltpu.SMEM)
-        row_z = jnp.pad(eigen_z, (0, 112), constant_values=1.0).reshape(1, 256)
+        hbm = pl.BlockSpec(memory_space=pltpu.HBM)
 
         def body(*refs):
             kernel(sizes, *refs)
@@ -596,13 +613,13 @@
         return pl.pallas_call(
             body,
             out_shape=jax.ShapeDtypeStruct((24, 24, 128), F32),
-            in_specs=[vmem] * 5 + [smem, smem, vmem],
+            in_specs=[hbm] * 5 + [smem] * 3,
             out_specs=vmem,
             scratch_shapes=scratch,
             compiler_params=pltpu.CompilerParams(
-                collective_id=0, has_side_effects=True, vmem_limit_bytes=40 * 1024 * 1024),
+                collective_id=0, has_side_effects=True, vmem_limit_bytes=60 * 1024 * 1024),
             cost_estimate=pl.CostEstimate(flops=1200000000, bytes_accessed=2000000, transcendentals=0),
-        )(right_side, reaction, basis_x, basis_y, basis_z, eigen_x, eigen_y, row_z)
+        )(right_side, reaction, basis_x, basis_y, basis_z, eigen_x, eigen_y, eigen_z)
 
     return jax.shard_map(
         local,

time: 108 us -> 89.1 us (0.82)
  Pallas kernels: 99.7 us -> 86.1 us
  local copies, waits for them, and re-layouts: 6.35 us -> 1.69 us
    pallas_call x1, Pallas kernels: 99.7 us -> 86.1 us  [local(): pl.pallas_call(body, out_shape=jax.ShapeDtypeStruct((24, 24, 128), F32),...]
    unnamed x15 -> x1, local copies, waits for them, and re-layouts: 5.67 us -> 1.69 us
where the time goes in v2:
time: 89.1 us; the launch traced here: 87.8 us
  Pallas kernels  86.1 us (97%)
  local copies, waits for them, and re-layouts  1.69 us (2%)
    pallas_call x1, Pallas kernels, local(): pl.pallas_call(body, out_shape=jax.ShapeDtypeStruct((24, 24, 128), F32),...  86.1 us

profile of v2, /device:TPU:7, one launch (start us, length us, event | category | flops | bytes accessed | tf_op | source)
XLA Modules:
  0.0 87.8 jit_solution(17029068174440319808)
XLA Ops:
  0.0 86.1 %shard_map.82 = f32[24,24,128]{2,1,0:T(8,128)} custom-call(f32[24,24,128]{2,1,0:T(8,128)} %refs_0_.1, f32[24,24,128]{2,1,0:T(8,128)} %refs_1_.1, f32[40,40]{1,0:T(8,128)} %refs_2_.1, f32[40,40]{1,0:T(8,128)} %refs_3_.1, f32[144,144]{1,0:T(8,128)} %refs_4_.1, f32[40]{0:T(128)} %refs_5_.1, f32[40]{0:T(128)} %refs_6_.1, f32[144]{0:T(256)} %refs_7_.1), custom_call_target="tpu_custom_call" | custom-call | flops 1200000000 | bytes 2000000 | tf_op jit(solution)/shard_map/pallas_call | solution.py:613
  86.1 1.7 %copy.10 = f32[24,24,128]{2,1,0:T(8,128)} copy(f32[24,24,128]{2,1,0:T(8,128)} %shard_map.82) | data formatting | bytes 589824

commit v3 on v2

v3 whole, which is shorter than its diff:
```python
import jax
import jax.numpy as jnp
from jax import lax
from jax.experimental import pallas as pl
from jax.experimental.pallas import tpu as pltpu
from jax.sharding import PartitionSpec as P

MESH = pl.DeviceIdType.MESH
F32 = jnp.float32
BF16 = jnp.bfloat16
DIRS = [(dy, dz) for dy in (-1, 0, 1) for dz in (-1, 0, 1) if (dy, dz) != (0, 0)]
STRAIGHT8, STRAIGHT17 = 5, 7


def split(x):
    hi = x.astype(BF16)
    return hi, (x - hi.astype(F32)).astype(BF16)


def mm(a, b):
    return lax.dot_general(a, b, (((1,), (0,)), ((), ())), preferred_element_type=F32)


def roll(x, shift):
    return pltpu.roll(x, shift % x.shape[-1], x.ndim - 1)


def kernel(sizes, f_hbm, rea_hbm, bx_hbm, by_hbm, bz_hbm, ex_hbm, ey_hbm, ez_hbm, out,
           f, rea, bx, by, bz, ex, ey, ez,
           E0, E1, RE0, RE1, T0, T1, U0, U1, V0, V1, inv, S,
           A0, A1, wz32, wxy32, wzf, wzb, wxf, wxb, wyf, wyb,
           pfA, pfB, pr, pmF, pmN, pvN, pvF, plF, plN, plO,
           rfA, rfB, rr, rmfF, rmfN, rmcF, rmcN, rmyF, rmyN, rvzN, rvzF, rvcN, rvcF, RN, RF, RRN, RRF,
           rlfF, rlfN, rlfO, rlcF, rlcN, rlcO, rlyF, rlyN, rlyO, X17, X2, RB8a, RB17, RB8b,
           ssem, rsem, lsem):
    n_gx, n_gy, n_gz = sizes
    gx, gy, gz = (lax.axis_index(a) for a in ("gx", "gy", "gz"))
    relay = n_gx == 8
    mid = n_gx // 2 - 1
    has_y = {-1: gy > 0, 0: gy >= 0, 1: gy < n_gy - 1}
    has_z = {-1: gz > 0, 0: gz >= 0, 1: gz < n_gz - 1}
    has_x = {-1: gx > 0, 1: gx < n_gx - 1}
    left = gx <= mid
    right = jnp.logical_not(left)

    def pick(a, b):
        return jnp.where(left, a, b)
    has = {d: has_y[d[0]] & has_z[d[1]] for d in DIRS}
    lane = lax.broadcasted_iota(jnp.int32, (8, 128), 1)
    sub = lax.broadcasted_iota(jnp.int32, (8, 128), 0)

    def lanes(rows):
        return lax.broadcasted_iota(jnp.int32, (rows, 128), 1)

    counter = [0]

    def slots(n):
        counter[0] += n
        return counter[0] - n

    def copy(k, src, dst, dev):
        return pltpu.make_async_remote_copy(
            src_ref=src, dst_ref=dst, send_sem=ssem.at[k], recv_sem=rsem.at[k],
            device_id=dev, device_id_type=MESH)

    class YZ:
        def __init__(self, items):
            self.items = {d: items(d) for d in DIRS}
            self.k = {d: slots(len(self.items[d])) for d in DIRS}

        def each(self, d, along):
            dev = (gx, gy + d[0], gz + d[1])
            for j, (src, dst) in enumerate(self.items[along]):
                yield copy(self.k[along] + j, src, dst, dev)

        def start(self):
            for d in DIRS:
                @pl.when(has[d])
                def _():
                    for c in self.each(d, d):
                        c.start()

        def wait(self):
            for d in DIRS:
                @pl.when(has[d])
                def _():
                    for c in self.each(d, (-d[0], -d[1])):
                        c.wait_recv()
                    for c in self.each(d, d):
                        c.wait_send()

    class XX:
        def __init__(self, srcs, dsts, layers, straight=None, rb=None):
            self.srcs, self.dsts, self.rb = srcs, dsts, rb
            self.layers, self.straight = layers, straight
            self.relayed = relay and straight is not None
            self.k = {s: slots(1) for s in (-1, 1)}
            if self.relayed:
                self.kr = slots(1)
                self.kp = {s: slots(4) for s in (-1, 1)}

        def end(self, s):
            return mid if s == 1 else mid + 1

        def via(self, s, j):
            return self.end(s) - s * j

        def whole(self, s):
            return copy(self.k[s], self.srcs[s], self.dsts[s], (gx + s, gy, gz))

        def cut(self, ref, j):
            if j == 0:
                return ref.at[pl.ds(0, self.straight)]
            return ref.at[pl.ds(self.straight, self.layers - self.straight), pl.ds(8 * (j - 1), 8)]

        def part(self, s, j):
            src = self.rb if j else self.cut(self.srcs[s], 0)
            return copy(self.kp[s] + j, src, self.cut(self.dsts[s], j), (self.end(s) + s, gy, gz))

        def leg(self, s, j):
            return pltpu.make_async_remote_copy(
                src_ref=self.cut(self.srcs[s], j), dst_ref=self.rb,
                send_sem=ssem.at[self.kp[s] + j], recv_sem=rsem.at[self.kr],
                device_id=(self.via(s, j), gy, gz), device_id_type=MESH)

        def start(self, s, cond):
            if not self.relayed:
                @pl.when(cond & has_x[s])
                def _():
                    self.whole(s).start()
                return

            @pl.when(cond & has_x[s] & (gx != self.end(s)))
            def _():
                self.whole(s).start()

            @pl.when(cond & (gx == self.end(s)))
            def _():
                for j in (1, 2, 3):
                    self.leg(s, j).start()
                self.part(s, 0).start()

        def forward(self):
            if self.relayed:
                for s in (1, -1):
                    for j in (1, 2, 3):
                        @pl.when(gx == self.via(s, j))
                        def _():
                            self.leg(s, j).wait_recv()
                            self.part(s, j).start()

        def arrive(self, s, cond):
            if not self.relayed:
                @pl.when(cond & has_x[-s])
                def _():
                    self.whole(s).wait_recv()
                return

            @pl.when(cond & has_x[-s] & (gx != self.end(s) + s))
            def _():
                self.whole(s).wait_recv()

            @pl.when(cond & (gx == self.end(s) + s))
            def _():
                for j in range(4):
                    self.part(s, j).wait_recv()

        def sent(self):
            for s in (1, -1):
                if not self.relayed:
                    @pl.when(has_x[s])
                    def _():
                        self.whole(s).wait_send()
                    continue

                @pl.when(has_x[s] & (gx != self.end(s)))
                def _():
                    self.whole(s).wait_send()

                @pl.when(gx == self.end(s))
                def _():
                    for j in (1, 2, 3):
                        self.leg(s, j).wait_send()
                    self.part(s, 0).wait_send()

                for j in (1, 2, 3):
                    @pl.when(gx == self.via(s, j))
                    def _():
                        self.part(s, j).wait_send()

        def start_far(self):
            self.start(1, left)
            self.start(-1, right)

        def start_near(self):
            self.start(-1, left)
            self.start(1, right)

        def arrive_near(self):
            self.arrive(1, left)
            self.arrive(-1, right)

        def arrive_far(self):
            self.arrive(-1, left)
            self.arrive(1, right)

    barrier = pltpu.get_barrier_semaphore()
    expect = jnp.int32(0)
    for d in DIRS:
        @pl.when(has[d])
        def _():
            pl.semaphore_signal(barrier, inc=1, device_id=(gx, gy + d[0], gz + d[1]), device_id_type=MESH)
        expect = expect + has[d].astype(jnp.int32)
    for s in (-1, 1):
        @pl.when(has_x[s])
        def _():
            pl.semaphore_signal(barrier, inc=1, device_id=(gx + s, gy, gz), device_id_type=MESH)
        expect = expect + has_x[s].astype(jnp.int32)
    if relay:
        pairs = []
        for s in (-1, 1):
            e = mid if s == 1 else mid + 1
            pairs += [(e, e - s * j) for j in (2, 3)] + [(e - s * j, e + s) for j in (1, 2, 3)]
        for a, b in pairs:
            for me, other in ((a, b), (b, a)):
                @pl.when(gx == me)
                def _():
                    pl.semaphore_signal(barrier, inc=1, device_id=(jnp.int32(other), gy, gz), device_id_type=MESH)
                expect = expect + (gx == me).astype(jnp.int32)

    loads = [pltpu.make_async_copy(a, b, lsem.at[i]) for i, (a, b) in enumerate(
        ((f_hbm, f), (bz_hbm, bz), (bx_hbm, bx), (by_hbm, by), (ex_hbm, ex), (ey_hbm, ey), (ez_hbm, ez), (rea_hbm, rea)))]
    for c in loads:
        c.start()
    for c in loads[:7]:
        c.wait()

    def edge(x, width):
        ln = lanes(x.shape[0])
        return jnp.where((ln < width) | (ln >= 128 - width), x, 0.0)

    def pack_one(dst, load, g, first, count, stride, masked):
        acc = None
        for i in range(count):
            x = load(first + i)
            if masked:
                x = edge(x, stride // 2)
            if i:
                x = roll(x, stride * i)
            acc = x if acc is None else acc + x
        dst[g] = acc

    def pack(dst, load, slabs, per, stride, masked):
        def body(g, c):
            pack_one(dst, load, g, g * per, per, stride, masked)
            return c
        full = slabs // per
        lax.fori_loop(0, full, body, 0)
        if slabs % per:
            pack_one(dst, load, full, full * per, slabs % per, stride, masked)

    def low_part(rows, stride):
        ln = lanes(rows)
        return (lax.rem(ln, stride) < stride // 2) & (ln < 128 - stride // 2 if stride == 18 else ln >= 0)

    def zero_missing(buf_of):
        for d in DIRS:
            bufs = buf_of(d)
            if bufs:
                @pl.when(jnp.logical_not(has[(-d[0], -d[1])]))
                def _():
                    for b in bufs:
                        b[...] = jnp.zeros(b.shape, F32)

    def halo_items(src, from0, x0, nx, dst, packed, recv, g0, groups):
        rows = {0: (0, 24, 0), 1: (16, 8, 32), -1: (0, 8, 24)}

        def items(d):
            s, n, t = rows[d[0]]
            if d[1] == 0:
                return [(src.at[pl.ds(from0, nx), pl.ds(s, n)], dst.at[pl.ds(x0, nx), pl.ds(t, n)])]
            return [(packed.at[pl.ds(g0, groups), pl.ds(s, n)],
                     recv.at[0 if d[1] == 1 else 1, pl.ds(g0, groups), pl.ds(t, n)])]
        return items

    def fold_items(a0, n, packed, recv_f, recv_c, recv_y):
        rows = {1: 24, -1: 32}

        def items(d):
            z = 0 if d[1] == 1 else 1
            y = 0 if d[0] == 1 else 1
            if d[1] == 0:
                return [(U0.at[pl.ds(a0, n), pl.ds(rows[d[0]], 8)], recv_y.at[y])]
            if d[0] == 0:
                return [(packed.at[:, pl.ds(0, 24)], recv_f.at[z])]
            return [(packed.at[:, pl.ds(rows[d[0]], 8)], recv_c.at[y, z])]
        return items

    def layer_items(v0, n, row_s, row_r, packed, recv_z, recv_c):
        def items(d):
            z = 0 if d[1] == 1 else 1
            y = 0 if d[0] == 1 else 1
            if d[1] == 0:
                s, t = ((16, 40), (0, 24))[y]
                return [(V0.at[pl.ds(v0, n), pl.ds(s, 8)], V0.at[pl.ds(v0, n), pl.ds(t, 8)]),
                        (row_s.at[y], row_r.at[y])]
            if d[0] == 0:
                return [(packed, recv_z.at[z])]
            return [(packed.at[:, pl.ds(8 if y == 0 else 0, 16)], recv_c.at[y, z])]
        return items

    def x_halo(b):
        return {1: b.at[pl.ds(32, 8), pl.ds(0, 24)], -1: b.at[pl.ds(24, 8), pl.ds(0, 24)]}

    def x_edge(b):
        return {1: b.at[pl.ds(16, 8)], -1: b.at[pl.ds(0, 8)]}

    xf = XX(x_edge(f), x_halo(E0), 8, STRAIGHT8, RB8a)
    xr = XX(x_edge(rea), x_halo(RE0), 8)
    xn, xfar = pick(32, 24), pick(24, 32)
    fA = YZ(halo_items(f, 0, 0, 24, E0, pfA, rfA, 0, 3))
    fN = YZ(halo_items(E0, xn, xn, 8, E0, pfB, rfB, 0, 1))
    fF = YZ(halo_items(E0, xfar, xfar, 8, E0, pfB, rfB, 1, 1))
    rA = YZ(halo_items(RE0, 0, 0, 40, RE0, pr, rr, 0, 5))
    aF, aN = pick(16, 0), pick(0, 24)
    m1F = YZ(fold_items(aF, 24, pmF, rmfF, rmcF, rmyF))
    m1N = YZ(fold_items(aN, 16, pmN, rmfN, rmcN, rmyN))
    m2 = XX({1: S.at[pl.ds(24, 17)], -1: S.at[pl.ds(1, 17)]}, {1: X17.at[0], -1: X17.at[1]}, 17, STRAIGHT17, RB17)
    vN, vF = pick(0, 17), pick(25, 0)
    m3N = YZ(layer_items(vN, 25, RN, RRN, pvN, rvzN, rvcN))
    m3F = YZ(layer_items(vF, 17, RF, RRF, pvF, rvzF, rvcF))
    eF, eN = pick(32, 0), pick(0, 32)
    l2F = YZ(fold_items(eF, 8, plF, rlfF, rlcF, rlyF))
    l2N = YZ(fold_items(eN, 8, plN, rlfN, rlcN, rlyN))
    l2O = YZ(fold_items(8, 24, plO, rlfO, rlcO, rlyO))
    x2 = XX({1: S.at[pl.ds(33, 8)], -1: S.at[pl.ds(1, 8)]}, {1: X2.at[0], -1: X2.at[1]}, 8, STRAIGHT8, RB8b)

    E0[pl.ds(0, 24), pl.ds(0, 24)] = f[...]
    pack(pfA, lambda i: f[i], 24, 8, 16, True)

    wz32[...] = jnp.zeros((256, 256), F32)
    wz32[0:128, 0:144] = bz[8:136, :]
    wz32[128:136, 0:144] = bz[136:144, :]
    wz32[248:256, 0:144] = bz[0:8, :]
    for w, table, turned in ((wzf, wz32[...], True), (wzb, wz32[...].T, False)):
        hi, lo = split(table)
        w[0:128] = hi[0:128]
        w[128:256] = hi[0:128]
        w[256:384] = lo[0:128]
        hi, lo = hi.astype(F32)[128:256], lo.astype(F32)[128:256]
        if turned:
            tail = jnp.concatenate([hi[0:8], hi[120:128], hi[0:8], lo[120:128], lo[0:8],
                                    jnp.zeros((80, 256), F32), hi[120:128]], axis=0)
        else:
            tail = jnp.concatenate([hi[0:16], hi[0:16], lo[0:16], jnp.zeros((80, 256), F32)], axis=0)
        w[384:512] = tail.astype(BF16)

    def blocks(w, m):
        wxy32[...] = jnp.zeros((80, 256), F32)
        hi, lo = split(m)
        hi, lo = hi.astype(F32), lo.astype(F32)
        for j, part in enumerate((hi, hi, lo)):
            wxy32[0:40, 80 * j:80 * j + 40] = part
            wxy32[40:80, 80 * j + 40:80 * j + 80] = part
        w[...] = wxy32[...].astype(BF16)

    x_nat, y_nat = bx[...], by[...]
    x_circ = jnp.concatenate([x_nat[8:40], x_nat[0:8]], axis=0)
    y_circ = jnp.concatenate([y_nat[8:40], y_nat[0:8]], axis=0)
    blocks(wxf, x_circ.T)
    blocks(wxb, x_nat)
    blocks(wyf, y_circ.T)
    blocks(wyb, y_circ)

    column = lax.broadcasted_iota(jnp.int32, (40, 128), 0)
    exc = lax.fori_loop(0, 40, lambda p, c: jnp.where(column == p, ex[p], c), jnp.zeros((40, 128), F32), unroll=8)
    ez0 = lax.fori_loop(0, 128, lambda p, c: jnp.where(lane == p, ez[p], c), jnp.ones((8, 128), F32), unroll=8)
    ez1 = lax.fori_loop(0, 16, lambda p, c: jnp.where(lane == p, ez[p + 128], c), jnp.ones((8, 128), F32), unroll=8)
    ez0, ez1 = (jnp.concatenate([e] * 5, axis=0) for e in (ez0, ez1))

    def table(q, c):
        base = exc + ey[q]
        inv[0, q] = 1.0 / (base + ez0)
        inv[1, q] = 1.0 / (base + ez1)
        return c
    lax.fori_loop(0, 40, table, 0, unroll=2)

    loads[7].wait()
    RE0[pl.ds(0, 24), pl.ds(0, 24)] = rea[...]

    def zrows(b, x0, nx, t):
        for i in range(nx // 8):
            b[pl.ds(x0 + 8 * i, 8), pl.ds(t, 8)] = jnp.zeros((8, 8, 128), F32)

    for s, x0 in ((-1, 32), (1, 24)):
        @pl.when(jnp.logical_not(has_x[s]))
        def _():
            for b in (E0, RE0):
                b[pl.ds(x0, 8), pl.ds(0, 24)] = jnp.zeros((8, 24, 128), F32)
            X17[0 if s == -1 else 1] = jnp.zeros((17, 24, 128), F32)
            X2[0 if s == -1 else 1] = jnp.zeros((8, 24, 128), F32)
    for s, t, tv in ((-1, 32, 40), (1, 24, 24)):
        @pl.when(jnp.logical_not(has_y[s]))
        def _():
            for b in (E0, RE0):
                zrows(b, 0, 40, t)
            zrows(V0, 0, 40, tv)
            V0[pl.ds(40, 2), pl.ds(tv, 8)] = jnp.zeros((2, 8, 128), F32)
            for b in (RRN, RRF, rmyF, rmyN, rlyF, rlyN, rlyO):
                b[0 if s == -1 else 1] = jnp.zeros(b.shape[1:], F32)

    def missing(d):
        z = 0 if d[1] == 1 else 1
        y = 0 if d[0] == 1 else 1
        t, n = {0: (0, 24), 1: (32, 8), -1: (24, 8)}[d[0]]
        if d[1] == 0:
            return []
        out_ = [b.at[z, :, pl.ds(t, n)] for b in (rfA, rfB, rr)]
        if d[0] == 0:
            return out_ + [b.at[z] for b in (rmfF, rmfN, rlfF, rlfN, rlfO, rvzN, rvzF)]
        return out_ + [b.at[y, z] for b in (rmcF, rmcN, rlcF, rlcN, rlcO, rvcN, rvcF)]
    zero_missing(missing)
    S[0] = jnp.zeros((24, 128), F32)
    S[41] = jnp.zeros((24, 128), F32)

    pl.semaphore_wait(barrier, expect)

    def unpack_group(recv, g, dst1, x0):
        both = jnp.where(low_part(40, 16), recv[1, g], recv[0, g])
        for i in range(8):
            dst1[x0 + i] = edge(roll(both, -16 * i), 8)

    def unpack_halo(recv, groups, dst1):
        def body(g, c):
            unpack_group(recv, g, dst1, 8 * g)
            return c
        lax.fori_loop(0, groups, body, 0)

    def cat3(x0, x1):
        h0, l0 = split(x0)
        h1 = x1.astype(BF16).astype(F32)
        l1 = x1 - h1
        tail = (h1 + roll(l1, 16) + roll(h1, 32)).astype(BF16)
        return jnp.concatenate([h0, l0, h0, tail], axis=1)

    def stack3(x):
        hi, lo = split(x)
        return jnp.concatenate([hi, lo, hi], axis=0)

    def forward_chunk(c, _):
        x0 = E0[pl.ds(8 * c, 8)].reshape(320, 128)
        x1 = E1[pl.ds(8 * c, 8)].reshape(320, 128)
        z = mm(cat3(x0, x1), wzf[...])
        for i in range(4):
            y = mm(wyf[:, 0:240], stack3(z[80 * i:80 * i + 80]))
            T0[pl.ds(320 * c + 80 * i, 80), :] = y[:, 0:128]
            T1[pl.ds(320 * c + 80 * i, 80), :] = y[:, 128:256]
        return _

    def middle(j, _):
        parts = []
        for i in range(2):
            q = 2 * j + i
            parts.append(jnp.concatenate([T0[pl.ds(q, 40, stride=40), :], T1[pl.ds(q, 40, stride=40), :]], axis=1))
        m = mm(wxf[:, 0:240], stack3(jnp.concatenate(parts, axis=0)))
        scale = jnp.concatenate([
            jnp.concatenate([inv[0, 2 * j + i], inv[1, 2 * j + i]], axis=1) for i in range(2)], axis=0)
        m = mm(wxb[:, 0:240], stack3(m * scale))
        for i in range(2):
            q = 2 * j + i
            T0[pl.ds(q, 40, stride=40), :] = m[40 * i:40 * i + 40, 0:128]
            T1[pl.ds(q, 40, stride=40), :] = m[40 * i:40 * i + 40, 128:256]
        return _

    def back_chunk(c, _):
        parts = []
        for i in range(4):
            x = jnp.concatenate([T0[pl.ds(320 * c + 80 * i, 80), :], T1[pl.ds(320 * c + 80 * i, 80), :]], axis=1)
            parts.append(mm(wyb[:, 0:240], stack3(x)))
        y = jnp.concatenate(parts, axis=0)
        z = mm(cat3(y[:, 0:128], y[:, 128:256]), wzb[...])
        U0[pl.ds(8 * c, 8)] = z[:, 0:128].reshape(8, 40, 128)
        U1[pl.ds(8 * c, 8)] = z[:, 128:256].reshape(8, 40, 128)
        return _

    def fold(a0, groups, recv_f, recv_c, recv_y):
        def body(g, c):
            both = jnp.where(low_part(24, 16), recv_f[0, g], recv_f[1, g])
            low = low_part(8, 16)
            first = jnp.where(low, recv_c[0, 0, g], recv_c[0, 1, g])
            last = jnp.where(low, recv_c[1, 0, g], recv_c[1, 1, g])
            both = both + jnp.concatenate([first, jnp.zeros((8, 128), F32), last], axis=0)
            for i in range(8):
                t = 8 * g + i
                zpart = edge(roll(both, -16 * i), 8)
                ypart = jnp.concatenate([recv_y[0, t], jnp.zeros((8, 128), F32), recv_y[1, t]], axis=0)
                S[a0 + t + 1] = U0[a0 + t, pl.ds(0, 24)] + (zpart + ypart)
            return c
        lax.fori_loop(0, groups, body, 0)

    def build(v0, side):
        def body(i, c):
            V0[v0 + i, pl.ds(0, 24)] = S[v0 + i] + X17[side, i]
            return c
        lax.fori_loop(0, 17, body, 0)

    def rows_out(rows, v0, n):
        rows[...] = jnp.zeros(rows.shape, F32)
        for i in range(n):
            rows[0, i:i + 1, :] = V0[v0 + i, 15:16, :]
            rows[1, i:i + 1, :] = V0[v0 + i, 8:9, :]

    def rows_in(rows, v0, n):
        for i in range(n):
            V0[v0 + i, 39:40, :] = rows[0, i:i + 1, :]
            V0[v0 + i, 32:33, :] = rows[1, i:i + 1, :]

    def unpack_layer(v0, n, recv_z, recv_c):
        def one(g, count):
            face = jnp.where(low_part(24, 18), recv_z[1, g], recv_z[0, g])
            low = low_part(16, 18)
            lo_y = jnp.where(low, recv_c[0, 1, g], recv_c[0, 0, g])
            hi_y = jnp.where(low, recv_c[1, 1, g], recv_c[1, 0, g])
            between = jnp.where(sub == 0, hi_y[8:16], lo_y[0:8])
            both = jnp.concatenate([face, hi_y[0:8], between, lo_y[8:16]], axis=0)
            for i in range(count):
                V1[v0 + g * 7 + i] = edge(roll(both, -18 * i), 9)

        def body(g, c):
            one(g, 7)
            return c
        lax.fori_loop(0, n // 7, body, 0)
        one(n // 7, n % 7)

    row = lax.broadcasted_iota(jnp.int32, (40, 128), 0)
    ln = lanes(40)
    inside_y = jnp.logical_not(((row >= 24) & (row < 32) & jnp.logical_not(has_y[1]))
                               | ((row >= 32) & jnp.logical_not(has_y[-1])))
    mask0 = jnp.where(inside_y, 1.0, 0.0)
    mask1 = jnp.where(inside_y & (((ln < 8) & has_z[1]) | ((ln >= 120) & has_z[-1])), 1.0, 0.0)
    ln48 = lanes(48)

    def shifts(v0, v1):
        p0, p1 = roll(v0, -1), roll(v1, -1)
        n0, n1 = roll(v0, 1), roll(v1, 1)
        top, bottom = ln48 == 127, ln48 == 0
        z0 = jnp.where(top, p1, p0) + jnp.where(bottom, n1, n0)
        z1 = jnp.where(top, p0, p1) + jnp.where(bottom, n0, n1)
        return z0 + 2.0 * v0, z1 + 2.0 * v1

    def ext(x):
        return jnp.concatenate([x[0:32], x[40:48]], axis=0)

    def level(v, c):
        A0[v], A1[v] = shifts(V0[v], V1[v])
        return c

    def stencil(a, c):
        x = jnp.where(a < 8, a + 32, a - 8)
        inside = jnp.where(((a < 8) & jnp.logical_not(has_x[-1])) | ((a >= 32) & jnp.logical_not(has_x[1])), 0.0, 1.0)
        for V, A, E, RE, m in ((V0, A0, E0, RE0, mask0), (V1, A1, E1, RE1, mask1)):
            v, z = V[a + 1], A[a + 1]
            total = A[a] + A[a + 2] + 2.0 * z
            along = 0.25 * v + 0.0625 * total
            k = 6.0 * v - 0.25 * (V[a] + V[a + 2] + z) - 0.125 * total
            k = k - (pltpu.roll(along, 47, 0) + pltpu.roll(along, 1, 0))
            E[x] = (E[x] - (RE[x] * ext(v) + ext(k))) * (m * inside)
        return c

    xf.start_far()
    xf.start_near()
    fA.start()
    xf.forward()
    fA.wait()
    unpack_halo(rfA, 3, E1)
    lax.fori_loop(0, 3, forward_chunk, 0, unroll=True)
    for arrive, x0, g, stage in ((xf.arrive_near, xn, 0, fN), (xf.arrive_far, xfar, 1, fF)):
        arrive()
        pack_one(pfB, lambda i: E0[x0 + i, pl.ds(0, 24)], g, 0, 8, 16, True)
        stage.start()
        if g:
            xr.start_far()
            xr.start_near()
        stage.wait()
        unpack_group(rfB, g, E1, x0)
        forward_chunk(x0 // 8, 0)
    xf.sent()
    lax.fori_loop(0, 20, middle, 0, unroll=10)
    bF, bN = pick(2, 0), pick(0, 3)
    lax.fori_loop(0, 3, lambda j, c: back_chunk(bF + j, c), 0, unroll=True)
    pack(pmF, lambda i: U1[aF + i], 24, 8, 16, False)
    m1F.start()
    lax.fori_loop(0, 2, lambda j, c: back_chunk(bN + j, c), 0, unroll=True)
    pack(pmN, lambda i: U1[aN + i], 16, 8, 16, False)
    m1N.start()
    m1F.wait()
    fold(aF, 3, rmfF, rmcF, rmyF)
    m2.start_far()
    m1N.wait()
    fold(aN, 2, rmfN, rmcN, rmyN)
    m2.start_near()
    m2.forward()

    m2.arrive_near()
    build(pick(0, 25), pick(0, 1))
    for i in range(8):
        V0[17 + i, pl.ds(0, 24)] = S[17 + i]
    for s, v in ((-1, 0), (1, 33)):
        @pl.when(jnp.logical_not(has_x[s]))
        def _():
            V0[pl.ds(v, 9), pl.ds(0, 24)] = jnp.zeros((9, 24, 128), F32)
    rows_out(RN, vN, 25)
    pack(pvN, lambda i: V0[vN + i, pl.ds(0, 24)], 25, 7, 18, True)
    m3N.start()
    xr.arrive_near()
    xr.arrive_far()
    xr.sent()
    pack(pr, lambda i: RE0[i, pl.ds(0, 24)], 40, 8, 16, True)
    rA.start()
    m3N.wait()
    rows_in(RRN, vN, 25)
    unpack_layer(vN, 25, rvzN, rvcN)
    l0 = pick(0, 18)
    lax.fori_loop(0, 24, lambda i, c: level(l0 + i, c), 0, unroll=3)
    rA.wait()
    unpack_halo(rr, 5, RE1)
    s0 = pick(0, 20)
    lax.fori_loop(0, 20, lambda i, c: stencil(s0 + i, c), 0, unroll=4)
    cN, cF = pick(0, 3), pick(2, 0)
    lax.fori_loop(0, 2, lambda j, c: forward_chunk(lax.rem(cN + j + 4, 5), c), 0, unroll=True)

    m2.arrive_far()
    m2.sent()
    build(pick(25, 0), pick(1, 0))
    rows_out(RF, vF, 17)
    pack(pvF, lambda i: V0[vF + i, pl.ds(0, 24)], 17, 7, 18, True)
    m3F.start()
    m3F.wait()
    rows_in(RRF, vF, 17)
    unpack_layer(vF, 17, rvzF, rvcF)
    l1 = pick(24, 0)
    lax.fori_loop(0, 18, lambda i, c: level(l1 + i, c), 0, unroll=3)
    s1 = pick(20, 0)
    lax.fori_loop(0, 20, lambda i, c: stencil(s1 + i, c), 0, unroll=4)

    lax.fori_loop(0, 3, lambda j, c: forward_chunk(lax.rem(cF + j + 4, 5), c), 0, unroll=True)
    lax.fori_loop(0, 20, middle, 0, unroll=10)
    for a0, packed, stage in ((eF, plF, l2F), (eN, plN, l2N)):
        back_chunk(a0 // 8, 0)
        pack_one(packed, lambda i: U1[a0 + i], 0, 0, 8, 16, False)
        stage.start()
    lax.fori_loop(1, 4, back_chunk, 0, unroll=True)
    l2F.wait()
    fold(eF, 1, rlfF, rlcF, rlyF)
    x2.start_far()
    pack(plO, lambda i: U1[i + 8], 24, 8, 16, False)
    l2O.start()
    l2N.wait()
    fold(eN, 1, rlfN, rlcN, rlyN)
    x2.start_near()
    x2.forward()
    l2O.wait()
    fold(8, 3, rlfO, rlcO, rlyO)
    x2.arrive_near()
    x2.arrive_far()
    x2.sent()

    def finish(i, c):
        out[i] = V0[i + 9, pl.ds(0, 24)] + (S[i + 9] + X2[0, i])
        out[i + 8] = V0[i + 17, pl.ds(0, 24)] + S[i + 17]
        out[i + 16] = V0[i + 25, pl.ds(0, 24)] + (S[i + 25] + X2[1, i])
        return c
    lax.fori_loop(0, 8, finish, 0)


def solution(mesh):
    sizes = tuple(mesh.shape[a] for a in ("gx", "gy", "gz"))

    def local(right_side, reaction, basis_x, basis_y, basis_z, eigen_x, eigen_y, eigen_z):
        def vm(*shape, dtype=F32):
            return pltpu.VMEM(shape, dtype)
        scratch = [vm(24, 24, 128), vm(24, 24, 128), vm(40, 40), vm(40, 40), vm(144, 144),
                   pltpu.SMEM((40,), F32), pltpu.SMEM((40,), F32), pltpu.SMEM((144,), F32)]
        scratch += [vm(40, 40, 128), vm(40, 40, 128), vm(40, 40, 128), vm(40, 40, 128),
                   vm(1600, 128), vm(1600, 128), vm(40, 40, 128), vm(40, 40, 128),
                   vm(42, 48, 128), vm(42, 48, 128), vm(2, 40, 40, 128), vm(42, 24, 128),
                   vm(42, 48, 128), vm(42, 48, 128),
                   vm(256, 256), vm(80, 256), vm(512, 256, dtype=BF16), vm(512, 256, dtype=BF16)]
        scratch += [vm(80, 256, dtype=BF16)] * 4
        scratch += [vm(3, 24, 128), vm(2, 24, 128), vm(5, 24, 128), vm(3, 40, 128), vm(2, 40, 128),
                    vm(4, 24, 128), vm(3, 24, 128), vm(1, 40, 128), vm(1, 40, 128), vm(3, 40, 128)]
        scratch += [vm(2, 3, 40, 128), vm(2, 2, 40, 128), vm(2, 5, 40, 128),
                    vm(2, 3, 24, 128), vm(2, 2, 24, 128), vm(2, 2, 3, 8, 128), vm(2, 2, 2, 8, 128),
                    vm(2, 24, 8, 128), vm(2, 16, 8, 128),
                    vm(2, 4, 24, 128), vm(2, 3, 24, 128), vm(2, 2, 4, 16, 128), vm(2, 2, 3, 16, 128),
                    vm(2, 32, 128), vm(2, 24, 128), vm(2, 32, 128), vm(2, 24, 128)]
        scratch += [vm(2, n, 24, 128) for n in (1, 1, 3)] + [vm(2, 2, n, 8, 128) for n in (1, 1, 3)]
        scratch += [vm(2, n, 8, 128) for n in (8, 8, 24)]
        scratch += [vm(2, 17, 24, 128), vm(2, 8, 24, 128),
                    vm(8 - STRAIGHT8, 8, 128), vm(17 - STRAIGHT17, 8, 128), vm(8 - STRAIGHT8, 8, 128),
                    pltpu.SemaphoreType.DMA((200,)), pltpu.SemaphoreType.DMA((200,)), pltpu.SemaphoreType.DMA((8,))]
        vmem = pl.BlockSpec(memory_space=pltpu.VMEM)
        hbm = pl.BlockSpec(memory_space=pltpu.HBM)

        def body(*refs):
            kernel(sizes, *refs)

        return pl.pallas_call(
            body,
            out_shape=jax.ShapeDtypeStruct((24, 24, 128), F32),
            in_specs=[hbm] * 8,
            out_specs=vmem,
            scratch_shapes=scratch,
            compiler_params=pltpu.CompilerParams(
                collective_id=0, has_side_effects=True, vmem_limit_bytes=40 * 1024 * 1024),
            cost_estimate=pl.CostEstimate(flops=1200000000, bytes_accessed=2000000, transcendentals=0),
        )(*(pltpu.with_memory_space_constraint(a, pltpu.HBM) for a in (
            right_side, reaction, basis_x, basis_y, basis_z, eigen_x, eigen_y, eigen_z)))

    return jax.shard_map(
        local,
        mesh=mesh,
        in_specs=(P("gx", "gy", "gz"), P("gx", "gy", "gz"), P(), P(), P(), P(), P(), P()),
        out_specs=P("gx", "gy", "gz"),
        check_vma=False,
    )
```

time: 89.1 us -> 88.9 us (level)
  local copies, waits for them, and re-layouts: 1.69 us -> 0.72 us
    unnamed x1, local copies, waits for them, and re-layouts: 1.69 us -> 0.72 us
where the time goes in v3:
time: 88.9 us; the launch traced here: 87.5 us
  Pallas kernels  86.8 us (98%)
    pallas_call x1, Pallas kernels, local(): pl.pallas_call(body, out_shape=jax.ShapeDtypeStruct((24, 24, 128), F32),...  86.8 us

profile of v3, /device:TPU:7, one launch (start us, length us, event | category | flops | bytes accessed | tf_op | source)
XLA Modules:
  0.0 87.5 jit_solution(2468543393357338697)
XLA Ops:
  0.0 86.8 %shard_map.82 = f32[24,24,128]{2,1,0:T(8,128)S(1)} custom-call(f32[24,24,128]{2,1,0:T(8,128)} %refs_0_.1, f32[24,24,128]{2,1,0:T(8,128)} %refs_1_.1, f32[40,40]{1,0:T(8,128)} %refs_2_.1, f32[40,40]{1,0:T(8,128)} %refs_3_.1, f32[144,144]{1,0:T(8,128)} %refs_4_.1, f32[40]{0:T(128)} %refs_5_.1, f32[40]{0:T(128)} %refs_6_.1, f32[144]{0:T(256)} %refs_7_.1), custom_call_target="tpu_custom_call" | custom-call | flops 1200000000 | bytes 2000000 | tf_op jit(solution)/shard_map/pallas_call | solution.py:708
  86.8 0.7 copy.10

commit v4 on v3

--- a/solution.py
+++ b/solution.py
@@ -9,7 +9,8 @@
 F32 = jnp.float32
 BF16 = jnp.bfloat16
 DIRS = [(dy, dz) for dy in (-1, 0, 1) for dz in (-1, 0, 1) if (dy, dz) != (0, 0)]
-STRAIGHT8, STRAIGHT17 = 5, 7
+STRAIGHT8, STRAIGHT17 = 2, 5
+PIECES = 3
 
 
 def split(x):
@@ -28,10 +29,10 @@
 def kernel(sizes, f_hbm, rea_hbm, bx_hbm, by_hbm, bz_hbm, ex_hbm, ey_hbm, ez_hbm, out,
            f, rea, bx, by, bz, ex, ey, ez,
            E0, E1, RE0, RE1, T0, T1, U0, U1, V0, V1, inv, S,
-           A0, A1, wz32, wxy32, wzf, wzb, wxf, wxb, wyf, wyb,
+           A0, A1, TP, invp, wz32, wxy32, wzf, wzb, wxf, wxb, wyf, wyb,
            pfA, pfB, pr, pmF, pmN, pvN, pvF, plF, plN, plO,
            rfA, rfB, rr, rmfF, rmfN, rmcF, rmcN, rmyF, rmyN, rvzN, rvzF, rvcN, rvcF, RN, RF, RRN, RRF,
-           rlfF, rlfN, rlfO, rlcF, rlcN, rlcO, rlyF, rlyN, rlyO, X17, X2, RB8a, RB17, RB8b,
+           rlfF, rlfN, rlfO, rlcF, rlcN, rlcO, rlyF, rlyN, rlyO, X17, X2, RB8a, RB17, RB8b, RB8c,
            ssem, rsem, lsem):
     n_gx, n_gy, n_gz = sizes
     gx, gy, gz = (lax.axis_index(a) for a in ("gx", "gy", "gz"))
@@ -96,8 +97,11 @@
             self.relayed = relay and straight is not None
             self.k = {s: slots(1) for s in (-1, 1)}
             if self.relayed:
-                self.kr = slots(1)
-                self.kp = {s: slots(4) for s in (-1, 1)}
+                self.kr = slots(PIECES)
+                self.kp = {s: slots(1 + 3 * PIECES) for s in (-1, 1)}
+                ends = [(layers - straight) * h // PIECES for h in range(PIECES + 1)]
+                self.pieces = [(a, b - a) for a, b in zip(ends[:-1], ends[1:])]
+                self.relays = [(j, h) for h in range(PIECES) for j in (1, 2, 3)]
 
         def end(self, s):
             return mid if s == 1 else mid + 1
@@ -108,19 +112,23 @@
         def whole(self, s):
             return copy(self.k[s], self.srcs[s], self.dsts[s], (gx + s, gy, gz))
 
-        def cut(self, ref, j):
+        def slot(self, s, j, h):
+            return self.kp[s] + (1 + 3 * h + j - 1 if j else 0)
+
+        def cut(self, ref, j, h):
             if j == 0:
                 return ref.at[pl.ds(0, self.straight)]
-            return ref.at[pl.ds(self.straight, self.layers - self.straight), pl.ds(8 * (j - 1), 8)]
-
-        def part(self, s, j):
-            src = self.rb if j else self.cut(self.srcs[s], 0)
-            return copy(self.kp[s] + j, src, self.cut(self.dsts[s], j), (self.end(s) + s, gy, gz))
-
-        def leg(self, s, j):
+            lo, n = self.pieces[h]
+            return ref.at[pl.ds(self.straight + lo, n), pl.ds(8 * (j - 1), 8)]
+
+        def part(self, s, j, h=0):
+            src = self.rb.at[pl.ds(*self.pieces[h])] if j else self.cut(self.srcs[s], 0, 0)
+            return copy(self.slot(s, j, h), src, self.cut(self.dsts[s], j, h), (self.end(s) + s, gy, gz))
+
+        def leg(self, s, j, h):
             return pltpu.make_async_remote_copy(
-                src_ref=self.cut(self.srcs[s], j), dst_ref=self.rb,
-                send_sem=ssem.at[self.kp[s] + j], recv_sem=rsem.at[self.kr],
+                src_ref=self.cut(self.srcs[s], j, h), dst_ref=self.rb.at[pl.ds(*self.pieces[h])],
+                send_sem=ssem.at[self.slot(s, j, h)], recv_sem=rsem.at[self.kr + h],
                 device_id=(self.via(s, j), gy, gz), device_id_type=MESH)
 
         def start(self, s, cond):
@@ -136,8 +144,8 @@
 
             @pl.when(cond & (gx == self.end(s)))
             def _():
-                for j in (1, 2, 3):
-                    self.leg(s, j).start()
+                for j, h in self.relays:
+                    self.leg(s, j, h).start()
                 self.part(s, 0).start()
 
         def forward(self):
@@ -146,8 +154,9 @@
                     for j in (1, 2, 3):
                         @pl.when(gx == self.via(s, j))
                         def _():
-                            self.leg(s, j).wait_recv()
-                            self.part(s, j).start()
+                            for h in range(PIECES):
+                                self.leg(s, j, h).wait_recv()
+                                self.part(s, j, h).start()
 
         def arrive(self, s, cond):
             if not self.relayed:
@@ -162,8 +171,9 @@
 
             @pl.when(cond & (gx == self.end(s) + s))
             def _():
-                for j in range(4):
-                    self.part(s, j).wait_recv()
+                self.part(s, 0).wait_recv()
+                for j, h in self.relays:
+                    self.part(s, j, h).wait_recv()
 
         def sent(self):
             for s in (1, -1):
@@ -179,14 +189,15 @@
 
                 @pl.when(gx == self.end(s))
                 def _():
-                    for j in (1, 2, 3):
-                        self.leg(s, j).wait_send()
+                    for j, h in self.relays:
+                        self.leg(s, j, h).wait_send()
                     self.part(s, 0).wait_send()
 
                 for j in (1, 2, 3):
                     @pl.when(gx == self.via(s, j))
                     def _():
-                        self.part(s, j).wait_send()
+                        for h in range(PIECES):
+                            self.part(s, j, h).wait_send()
 
         def start_far(self):
             self.start(1, left)
@@ -316,7 +327,7 @@
         return {1: b.at[pl.ds(16, 8)], -1: b.at[pl.ds(0, 8)]}
 
     xf = XX(x_edge(f), x_halo(E0), 8, STRAIGHT8, RB8a)
-    xr = XX(x_edge(rea), x_halo(RE0), 8)
+    xr = XX(x_edge(rea), x_halo(RE0), 8, STRAIGHT8, RB8c)
     xn, xfar = pick(32, 24), pick(24, 32)
     fA = YZ(halo_items(f, 0, 0, 24, E0, pfA, rfA, 0, 3))
     fN = YZ(halo_items(E0, xn, xn, 8, E0, pfB, rfB, 0, 1))
@@ -378,12 +389,20 @@
     ez1 = lax.fori_loop(0, 16, lambda p, c: jnp.where(lane == p, ez[p + 128], c), jnp.ones((8, 128), F32), unroll=8)
     ez0, ez1 = (jnp.concatenate([e] * 5, axis=0) for e in (ez0, ez1))
 
-    def table(q, c):
-        base = exc + ey[q]
-        inv[0, q] = 1.0 / (base + ez0)
-        inv[1, q] = 1.0 / (base + ez1)
+    first16 = lanes(40) < 16
+
+    def table(g, c):
+        acc = None
+        for i in range(8):
+            base = exc + ey[8 * g + i]
+            inv[8 * g + i] = 1.0 / (base + ez0)
+            tail = jnp.where(first16, 1.0 / (base + ez1), 0.0)
+            acc = tail if acc is None else acc + roll(tail, 16 * i)
+        invp[g] = acc
         return c
-    lax.fori_loop(0, 40, table, 0, unroll=2)
+    lax.fori_loop(0, 5, table, 0)
+    invp[5] = jnp.zeros((40, 128), F32)
+    TP[5] = jnp.zeros((40, 128), F32)
 
     loads[7].wait()
     RE0[pl.ds(0, 24), pl.ds(0, 24)] = rea[...]
@@ -457,20 +476,36 @@
             T1[pl.ds(320 * c + 80 * i, 80), :] = y[:, 128:256]
         return _
 
-    def middle(j, _):
-        parts = []
-        for i in range(2):
-            q = 2 * j + i
-            parts.append(jnp.concatenate([T0[pl.ds(q, 40, stride=40), :], T1[pl.ds(q, 40, stride=40), :]], axis=1))
-        m = mm(wxf[:, 0:240], stack3(jnp.concatenate(parts, axis=0)))
-        scale = jnp.concatenate([
-            jnp.concatenate([inv[0, 2 * j + i], inv[1, 2 * j + i]], axis=1) for i in range(2)], axis=0)
+    def four(load):
+        x = [load(i) for i in range(4)]
+        return jnp.concatenate([jnp.concatenate(x[0:2], axis=0), jnp.concatenate(x[2:4], axis=0)], axis=1)
+
+    def divide(x, scale):
+        m = mm(wxf[:, 0:240], stack3(x))
         m = mm(wxb[:, 0:240], stack3(m * scale))
-        for i in range(2):
-            q = 2 * j + i
-            T0[pl.ds(q, 40, stride=40), :] = m[40 * i:40 * i + 40, 0:128]
-            T1[pl.ds(q, 40, stride=40), :] = m[40 * i:40 * i + 40, 128:256]
-        return _
+        return [m[40 * (i % 2):40 * (i % 2) + 40, 128 * (i // 2):128 * (i // 2) + 128] for i in range(4)]
+
+    def middle():
+        def at(q):
+            return pl.ds(q, 40, stride=40)
+
+        def group(g, c):
+            acc = None
+            for i in range(8):
+                t = T1[at(8 * g + i), :]
+                acc = t if acc is None else acc + roll(t, 16 * i)
+            TP[g] = acc
+            for h in range(2):
+                q = 8 * g + 4 * h
+                for i, m in enumerate(divide(four(lambda i: T0[at(q + i), :]), four(lambda i: inv[q + i]))):
+                    T0[at(q + i), :] = m
+            return c
+        lax.fori_loop(0, 5, group, 0, unroll=True)
+        tails = divide(four(lambda i: TP[i]), four(lambda i: invp[i]))
+        tails += divide(four(lambda i: TP[4 if i == 0 else 5]), four(lambda i: invp[4 if i == 0 else 5]))[0:1]
+        for g in range(5):
+            for i in range(8):
+                T1[at(8 * g + i), :] = jnp.where(first16, roll(tails[g], -16 * i), 0.0)
 
     def back_chunk(c, _):
         parts = []
@@ -585,7 +620,7 @@
         unpack_group(rfB, g, E1, x0)
         forward_chunk(x0 // 8, 0)
     xf.sent()
-    lax.fori_loop(0, 20, middle, 0, unroll=10)
+    middle()
     bF, bN = pick(2, 0), pick(0, 3)
     lax.fori_loop(0, 3, lambda j, c: back_chunk(bF + j, c), 0, unroll=True)
     pack(pmF, lambda i: U1[aF + i], 24, 8, 16, False)
@@ -593,6 +628,7 @@
     lax.fori_loop(0, 2, lambda j, c: back_chunk(bN + j, c), 0, unroll=True)
     pack(pmN, lambda i: U1[aN + i], 16, 8, 16, False)
     m1N.start()
+    xr.forward()
     m1F.wait()
     fold(aF, 3, rmfF, rmcF, rmyF)
     m2.start_far()
@@ -644,7 +680,7 @@
     lax.fori_loop(0, 20, lambda i, c: stencil(s1 + i, c), 0, unroll=4)
 
     lax.fori_loop(0, 3, lambda j, c: forward_chunk(lax.rem(cF + j + 4, 5), c), 0, unroll=True)
-    lax.fori_loop(0, 20, middle, 0, unroll=10)
+    middle()
     for a0, packed, stage in ((eF, plF, l2F), (eN, plN, l2N)):
         back_chunk(a0 // 8, 0)
         pack_one(packed, lambda i: U1[a0 + i], 0, 0, 8, 16, False)
@@ -683,8 +719,8 @@
                    pltpu.SMEM((40,), F32), pltpu.SMEM((40,), F32), pltpu.SMEM((144,), F32)]
         scratch += [vm(40, 40, 128), vm(40, 40, 128), vm(40, 40, 128), vm(40, 40, 128),
                    vm(1600, 128), vm(1600, 128), vm(40, 40, 128), vm(40, 40, 128),
-                   vm(42, 48, 128), vm(42, 48, 128), vm(2, 40, 40, 128), vm(42, 24, 128),
-                   vm(42, 48, 128), vm(42, 48, 128),
+                   vm(42, 48, 128), vm(42, 48, 128), vm(40, 40, 128), vm(42, 24, 128),
+                   vm(42, 48, 128), vm(42, 48, 128), vm(6, 40, 128), vm(6, 40, 128),
                    vm(256, 256), vm(80, 256), vm(512, 256, dtype=BF16), vm(512, 256, dtype=BF16)]
         scratch += [vm(80, 256, dtype=BF16)] * 4
         scratch += [vm(3, 24, 128), vm(2, 24, 128), vm(5, 24, 128), vm(3, 40, 128), vm(2, 40, 128),
@@ -697,8 +733,8 @@
         scratch += [vm(2, n, 24, 128) for n in (1, 1, 3)] + [vm(2, 2, n, 8, 128) for n in (1, 1, 3)]
         scratch += [vm(2, n, 8, 128) for n in (8, 8, 24)]
         scratch += [vm(2, 17, 24, 128), vm(2, 8, 24, 128),
-                    vm(8 - STRAIGHT8, 8, 128), vm(17 - STRAIGHT17, 8, 128), vm(8 - STRAIGHT8, 8, 128),
-                    pltpu.SemaphoreType.DMA((200,)), pltpu.SemaphoreType.DMA((200,)), pltpu.SemaphoreType.DMA((8,))]
+                    vm(8 - STRAIGHT8, 8, 128), vm(17 - STRAIGHT17, 8, 128), vm(8 - STRAIGHT8, 8, 128), vm(8 - STRAIGHT8, 8, 128),
+                    pltpu.SemaphoreType.DMA((240,)), pltpu.SemaphoreType.DMA((240,)), pltpu.SemaphoreType.DMA((8,))]
         vmem = pl.BlockSpec(memory_space=pltpu.VMEM)
         hbm = pl.BlockSpec(memory_space=pltpu.HBM)
 

time: 88.9 us -> 81.2 us (0.913); the launches traced: 87.5 us -> 81 us
  Pallas kernels: 86.8 us -> 80.3 us
    pallas_call x1, Pallas kernels: 86.8 us -> 80.3 us  [local(): pl.pallas_call(body, out_shape=jax.ShapeDtypeStruct((24, 24, 128), F32),...]
where the time goes in v4:
time: 81.2 us; the launch traced here: 81 us
  Pallas kernels  80.3 us (99%)
    pallas_call x1, Pallas kernels, local(): pl.pallas_call(body, out_shape=jax.ShapeDtypeStruct((24, 24, 128), F32),...  80.3 us

profile of v4, /device:TPU:7, one launch (start us, length us, event | category | flops | bytes accessed | tf_op | source)
XLA Modules:
  0.0 81.0 jit_solution(17869176765360895015)
XLA Ops:
  0.0 80.3 %shard_map.82 = f32[24,24,128]{2,1,0:T(8,128)S(1)} custom-call(f32[24,24,128]{2,1,0:T(8,128)} %refs_0_.1, f32[24,24,128]{2,1,0:T(8,128)} %refs_1_.1, f32[40,40]{1,0:T(8,128)} %refs_2_.1, f32[40,40]{1,0:T(8,128)} %refs_3_.1, f32[144,144]{1,0:T(8,128)} %refs_4_.1, f32[40]{0:T(128)} %refs_5_.1, f32[40]{0:T(128)} %refs_6_.1, f32[144]{0:T(256)} %refs_7_.1), custom_call_target="tpu_custom_call" | custom-call | flops 1200000000 | bytes 2000000 | tf_op jit(solution)/shard_map/pallas_call | solution.py:744
  80.3 0.7 copy.10

commit v5 on v4

--- a/solution.py
+++ b/solution.py
@@ -8,8 +8,8 @@
 MESH = pl.DeviceIdType.MESH
 F32 = jnp.float32
 BF16 = jnp.bfloat16
-DIRS = [(dy, dz) for dy in (-1, 0, 1) for dz in (-1, 0, 1) if (dy, dz) != (0, 0)]
-STRAIGHT8, STRAIGHT17 = 2, 5
+DIRS = [(-1, 0), (1, 0), (0, -1), (0, 1), (-1, -1), (-1, 1), (1, -1), (1, 1)]
+STRAIGHT8, STRAIGHT16 = 3, 5
 PIECES = 3
 
 
@@ -32,7 +32,7 @@
            A0, A1, TP, invp, wz32, wxy32, wzf, wzb, wxf, wxb, wyf, wyb,
            pfA, pfB, pr, pmF, pmN, pvN, pvF, plF, plN, plO,
            rfA, rfB, rr, rmfF, rmfN, rmcF, rmcN, rmyF, rmyN, rvzN, rvzF, rvcN, rvcF, RN, RF, RRN, RRF,
-           rlfF, rlfN, rlfO, rlcF, rlcN, rlcO, rlyF, rlyN, rlyO, X17, X2, RB8a, RB17, RB8b, RB8c,
+           rlfF, rlfN, rlfO, rlcF, rlcN, rlcO, rlyF, rlyN, rlyO, X17, X2, RB8a, RB16, RB8b, RB8c,
            ssem, rsem, lsem):
     n_gx, n_gy, n_gz = sizes
     gx, gy, gz = (lax.axis_index(a) for a in ("gx", "gy", "gz"))
@@ -81,12 +81,17 @@
                     for c in self.each(d, d):
                         c.start()
 
-        def wait(self):
+        def arrive(self):
             for d in DIRS:
                 @pl.when(has[d])
                 def _():
                     for c in self.each(d, (-d[0], -d[1])):
                         c.wait_recv()
+
+        def sent(self):
+            for d in DIRS:
+                @pl.when(has[d])
+                def _():
                     for c in self.each(d, d):
                         c.wait_send()
 
@@ -233,11 +238,10 @@
             e = mid if s == 1 else mid + 1
             pairs += [(e, e - s * j) for j in (2, 3)] + [(e - s * j, e + s) for j in (1, 2, 3)]
         for a, b in pairs:
-            for me, other in ((a, b), (b, a)):
-                @pl.when(gx == me)
-                def _():
-                    pl.semaphore_signal(barrier, inc=1, device_id=(jnp.int32(other), gy, gz), device_id_type=MESH)
-                expect = expect + (gx == me).astype(jnp.int32)
+            @pl.when(gx == b)
+            def _():
+                pl.semaphore_signal(barrier, inc=1, device_id=(jnp.int32(a), gy, gz), device_id_type=MESH)
+            expect = expect + (gx == a).astype(jnp.int32)
 
     loads = [pltpu.make_async_copy(a, b, lsem.at[i]) for i, (a, b) in enumerate(
         ((f_hbm, f), (bz_hbm, bz), (bx_hbm, bx), (by_hbm, by), (ex_hbm, ex), (ey_hbm, ey), (ez_hbm, ez), (rea_hbm, rea)))]
@@ -333,10 +337,13 @@
     fN = YZ(halo_items(E0, xn, xn, 8, E0, pfB, rfB, 0, 1))
     fF = YZ(halo_items(E0, xfar, xfar, 8, E0, pfB, rfB, 1, 1))
     rA = YZ(halo_items(RE0, 0, 0, 40, RE0, pr, rr, 0, 5))
-    aF, aN = pick(16, 0), pick(0, 24)
-    m1F = YZ(fold_items(aF, 24, pmF, rmfF, rmcF, rmyF))
-    m1N = YZ(fold_items(aN, 16, pmN, rmfN, rmcN, rmyN))
-    m2 = XX({1: S.at[pl.ds(24, 17)], -1: S.at[pl.ds(1, 17)]}, {1: X17.at[0], -1: X17.at[1]}, 17, STRAIGHT17, RB17)
+    aF, aN = pick(24, 0), pick(0, 16)
+    m1F = YZ(fold_items(aF, 16, pmF, rmfF, rmcF, rmyF))
+    m1N = YZ(fold_items(aN, 24, pmN, rmfN, rmcN, rmyN))
+    m2 = XX({1: S.at[pl.ds(25, 16)], -1: S.at[pl.ds(1, 16)]},
+            {1: X17.at[0, pl.ds(1, 16)], -1: X17.at[1, pl.ds(0, 16)]}, 16, STRAIGHT16, RB16)
+    m2b = XX({1: S.at[pl.ds(24, 1)], -1: S.at[pl.ds(17, 1)]},
+             {1: X17.at[0, pl.ds(0, 1)], -1: X17.at[1, pl.ds(16, 1)]}, 1)
     vN, vF = pick(0, 17), pick(25, 0)
     m3N = YZ(layer_items(vN, 25, RN, RRN, pvN, rvzN, rvcN))
     m3F = YZ(layer_items(vF, 17, RF, RRF, pvF, rvzF, rvcF))
@@ -606,7 +613,7 @@
     xf.start_near()
     fA.start()
     xf.forward()
-    fA.wait()
+    fA.arrive()
     unpack_halo(rfA, 3, E1)
     lax.fori_loop(0, 3, forward_chunk, 0, unroll=True)
     for arrive, x0, g, stage in ((xf.arrive_near, xn, 0, fN), (xf.arrive_far, xfar, 1, fF)):
@@ -616,28 +623,30 @@
         if g:
             xr.start_far()
             xr.start_near()
-        stage.wait()
+        stage.arrive()
         unpack_group(rfB, g, E1, x0)
         forward_chunk(x0 // 8, 0)
-    xf.sent()
     middle()
-    bF, bN = pick(2, 0), pick(0, 3)
-    lax.fori_loop(0, 3, lambda j, c: back_chunk(bF + j, c), 0, unroll=True)
-    pack(pmF, lambda i: U1[aF + i], 24, 8, 16, False)
+    bF, bN = pick(3, 0), pick(0, 2)
+    lax.fori_loop(0, 2, lambda j, c: back_chunk(bF + j, c), 0, unroll=True)
+    pack(pmF, lambda i: U1[aF + i], 16, 8, 16, False)
     m1F.start()
-    lax.fori_loop(0, 2, lambda j, c: back_chunk(bN + j, c), 0, unroll=True)
-    pack(pmN, lambda i: U1[aN + i], 16, 8, 16, False)
+    lax.fori_loop(0, 3, lambda j, c: back_chunk(bN + j, c), 0, unroll=True)
+    pack(pmN, lambda i: U1[aN + i], 24, 8, 16, False)
     m1N.start()
     xr.forward()
-    m1F.wait()
-    fold(aF, 3, rmfF, rmcF, rmyF)
+    m1F.arrive()
+    fold(aF, 2, rmfF, rmcF, rmyF)
     m2.start_far()
-    m1N.wait()
-    fold(aN, 2, rmfN, rmcN, rmyN)
+    m1N.arrive()
+    fold(aN, 3, rmfN, rmcN, rmyN)
+    m2b.start_far()
     m2.start_near()
+    m2b.start_near()
     m2.forward()
 
     m2.arrive_near()
+    m2b.arrive_near()
     build(pick(0, 25), pick(0, 1))
     for i in range(8):
         V0[17 + i, pl.ds(0, 24)] = S[17 + i]
@@ -650,34 +659,35 @@
     m3N.start()
     xr.arrive_near()
     xr.arrive_far()
-    xr.sent()
     pack(pr, lambda i: RE0[i, pl.ds(0, 24)], 40, 8, 16, True)
     rA.start()
-    m3N.wait()
+    m3N.arrive()
+    for stage in (fA, fN, fF, xf, m1F, m1N):
+        stage.sent()
     rows_in(RRN, vN, 25)
     unpack_layer(vN, 25, rvzN, rvcN)
     l0 = pick(0, 18)
     lax.fori_loop(0, 24, lambda i, c: level(l0 + i, c), 0, unroll=3)
-    rA.wait()
+    rA.arrive()
     unpack_halo(rr, 5, RE1)
-    s0 = pick(0, 20)
-    lax.fori_loop(0, 20, lambda i, c: stencil(s0 + i, c), 0, unroll=4)
+    s0 = pick(0, 18)
+    lax.fori_loop(0, 22, lambda i, c: stencil(s0 + i, c), 0, unroll=2)
     cN, cF = pick(0, 3), pick(2, 0)
     lax.fori_loop(0, 2, lambda j, c: forward_chunk(lax.rem(cN + j + 4, 5), c), 0, unroll=True)
 
     m2.arrive_far()
-    m2.sent()
+    m2b.arrive_far()
     build(pick(25, 0), pick(1, 0))
     rows_out(RF, vF, 17)
     pack(pvF, lambda i: V0[vF + i, pl.ds(0, 24)], 17, 7, 18, True)
     m3F.start()
-    m3F.wait()
+    m3F.arrive()
     rows_in(RRF, vF, 17)
     unpack_layer(vF, 17, rvzF, rvcF)
     l1 = pick(24, 0)
     lax.fori_loop(0, 18, lambda i, c: level(l1 + i, c), 0, unroll=3)
-    s1 = pick(20, 0)
-    lax.fori_loop(0, 20, lambda i, c: stencil(s1 + i, c), 0, unroll=4)
+    s1 = pick(22, 0)
+    lax.fori_loop(0, 18, lambda i, c: stencil(s1 + i, c), 0, unroll=6)
 
     lax.fori_loop(0, 3, lambda j, c: forward_chunk(lax.rem(cF + j + 4, 5), c), 0, unroll=True)
     middle()
@@ -686,20 +696,21 @@
         pack_one(packed, lambda i: U1[a0 + i], 0, 0, 8, 16, False)
         stage.start()
     lax.fori_loop(1, 4, back_chunk, 0, unroll=True)
-    l2F.wait()
+    m2.sent()
+    m2b.sent()
+    l2F.arrive()
     fold(eF, 1, rlfF, rlcF, rlyF)
     x2.start_far()
     pack(plO, lambda i: U1[i + 8], 24, 8, 16, False)
     l2O.start()
-    l2N.wait()
+    l2N.arrive()
     fold(eN, 1, rlfN, rlcN, rlyN)
     x2.start_near()
     x2.forward()
-    l2O.wait()
+    l2O.arrive()
     fold(8, 3, rlfO, rlcO, rlyO)
     x2.arrive_near()
     x2.arrive_far()
-    x2.sent()
 
     def finish(i, c):
         out[i] = V0[i + 9, pl.ds(0, 24)] + (S[i + 9] + X2[0, i])
@@ -707,6 +718,8 @@
         out[i + 16] = V0[i + 25, pl.ds(0, 24)] + (S[i + 25] + X2[1, i])
         return c
     lax.fori_loop(0, 8, finish, 0)
+    for stage in (rA, m3N, m3F, l2F, l2N, l2O, xr, x2):
+        stage.sent()
 
 
 def solution(mesh):
@@ -723,17 +736,17 @@
                    vm(42, 48, 128), vm(42, 48, 128), vm(6, 40, 128), vm(6, 40, 128),
                    vm(256, 256), vm(80, 256), vm(512, 256, dtype=BF16), vm(512, 256, dtype=BF16)]
         scratch += [vm(80, 256, dtype=BF16)] * 4
-        scratch += [vm(3, 24, 128), vm(2, 24, 128), vm(5, 24, 128), vm(3, 40, 128), vm(2, 40, 128),
+        scratch += [vm(3, 24, 128), vm(2, 24, 128), vm(5, 24, 128), vm(2, 40, 128), vm(3, 40, 128),
                     vm(4, 24, 128), vm(3, 24, 128), vm(1, 40, 128), vm(1, 40, 128), vm(3, 40, 128)]
         scratch += [vm(2, 3, 40, 128), vm(2, 2, 40, 128), vm(2, 5, 40, 128),
-                    vm(2, 3, 24, 128), vm(2, 2, 24, 128), vm(2, 2, 3, 8, 128), vm(2, 2, 2, 8, 128),
-                    vm(2, 24, 8, 128), vm(2, 16, 8, 128),
+                    vm(2, 2, 24, 128), vm(2, 3, 24, 128), vm(2, 2, 2, 8, 128), vm(2, 2, 3, 8, 128),
+                    vm(2, 16, 8, 128), vm(2, 24, 8, 128),
                     vm(2, 4, 24, 128), vm(2, 3, 24, 128), vm(2, 2, 4, 16, 128), vm(2, 2, 3, 16, 128),
                     vm(2, 32, 128), vm(2, 24, 128), vm(2, 32, 128), vm(2, 24, 128)]
         scratch += [vm(2, n, 24, 128) for n in (1, 1, 3)] + [vm(2, 2, n, 8, 128) for n in (1, 1, 3)]
         scratch += [vm(2, n, 8, 128) for n in (8, 8, 24)]
         scratch += [vm(2, 17, 24, 128), vm(2, 8, 24, 128),
-                    vm(8 - STRAIGHT8, 8, 128), vm(17 - STRAIGHT17, 8, 128), vm(8 - STRAIGHT8, 8, 128), vm(8 - STRAIGHT8, 8, 128),
+                    vm(8 - STRAIGHT8, 8, 128), vm(16 - STRAIGHT16, 8, 128), vm(8 - STRAIGHT8, 8, 128), vm(8 - STRAIGHT8, 8, 128),
                     pltpu.SemaphoreType.DMA((240,)), pltpu.SemaphoreType.DMA((240,)), pltpu.SemaphoreType.DMA((8,))]
         vmem = pl.BlockSpec(memory_space=pltpu.VMEM)
         hbm = pl.BlockSpec(memory_space=pltpu.HBM)

time: 81.2 us -> 80.2 us (0.988)
  Pallas kernels: 80.3 us -> 79.3 us
    pallas_call x1, Pallas kernels: 80.3 us -> 79.3 us  [local(): pl.pallas_call(body, out_shape=jax.ShapeDtypeStruct((24, 24, 128), F32),...]
where the time goes in v5:
time: 80.2 us; the launch traced here: 80 us
  Pallas kernels  79.3 us (99%)
    pallas_call x1, Pallas kernels, local(): pl.pallas_call(body, out_shape=jax.ShapeDtypeStruct((24, 24, 128), F32),...  79.3 us

profile of v5, /device:TPU:7, one launch (start us, length us, event | category | flops | bytes accessed | tf_op | source)
XLA Modules:
  0.0 80.0 jit_solution(5898573444921736679)
XLA Ops:
  0.0 79.3 %shard_map.82 = f32[24,24,128]{2,1,0:T(8,128)S(1)} custom-call(f32[24,24,128]{2,1,0:T(8,128)} %refs_0_.1, f32[24,24,128]{2,1,0:T(8,128)} %refs_1_.1, f32[40,40]{1,0:T(8,128)} %refs_2_.1, f32[40,40]{1,0:T(8,128)} %refs_3_.1, f32[144,144]{1,0:T(8,128)} %refs_4_.1, f32[40]{0:T(128)} %refs_5_.1, f32[40]{0:T(128)} %refs_6_.1, f32[144]{0:T(256)} %refs_7_.1), custom_call_target="tpu_custom_call" | custom-call | flops 1200000000 | bytes 2000000 | tf_op jit(solution)/shard_map/pallas_call | solution.py:757
  79.3 0.7 copy.10
